TPU v7x, 256 devices: a whole 4x4x8 slice. The times are simulated.
256 devices in a mesh: dp: 4 (over y), expert: 64 (over z, x, core).
Axes of the slice: x: 4, y: 4, z: 8, core: 2. Of those that a mesh axis runs over, the one named last changes fastest.
Arguments:
- tokens: bfloat16 [32768, 2048], P(('dp', 'expert')), may hold values from -6 to 6
- cotangent: bfloat16 [32768, 2048], P(('dp', 'expert')), may hold values from -6 to 6
- expert_ids: int32 [32768, 8], P(('dp', 'expert')), may hold values from 0 to 63, all different within a row; in each aligned block of 128 rows (0 to 127, 128 to 255, ...) at most 24 rows name the same one
- gate_probs: float32 [32768, 8], P(('dp', 'expert')), may hold values from 0.05 to 1
- up_weight: bfloat16 [64, 2048, 768], P('expert', None, 'dp'), may hold values from -0.125 to 0.125
- down_weight: float32 [64, 768, 2048], P('expert', 'dp'), may hold values from -28 to 28
- moment1: float32 [64, 768, 2048], P('expert', 'dp'), may hold values from -60 to 60
- moment2: float32 [64, 768, 2048], P('expert', 'dp'), may hold values from 0.05 to 5
- pair_match: int32 [64], replicated, may hold values from 0 to 63, as said below
Outputs:
- down_out: float32 [64, 768, 2048], P('expert', 'dp')
- moment1_out: float32 [64, 768, 2048], P('expert', 'dp')
- moment2_out: float32 [64, 768, 2048], P('expert', 'dp')
Inputs may be any that keep to these rules, and one draw needn't show every extreme that they name: `expert_ids`: each row names 8 different experts. Within the rows of one device (aligned blocks of 128 rows) no expert is named by more than 24 rows, a bound that some block reaches. A perfect matching: pair_match[pair_match[i]] = i and pair_match[i] != i for every i.
All inputs are finite; a program needn't handle non-finite values.
Results may differ from a plain program's by a relative error of at most 0.00035.
Values may be sent and summed in bfloat16 or wider, within the bound.
A program may use at most 128 MiB of HBM per device.

v0:
```python
import jax
import jax.numpy as jnp
from jax import lax
from jax.sharding import PartitionSpec as P

beta_one = 0.9
beta_two = 0.999
epsilon = 1e-06
learn_rate = 0.05


def relocate(states, pair_match):
    group_size = lax.axis_size("expert")
    count_states = len(states)
    stacked = jnp.stack(states).reshape(count_states, group_size, -1)
    chosen = jnp.take(
        lax.all_to_all(stacked, "expert", split_axis=1, concat_axis=1, tiled=True),
        pair_match,
        axis=1,
    )
    arrived = lax.all_to_all(chosen, "expert", split_axis=1, concat_axis=1, tiled=True)
    arrived = arrived.reshape((count_states,) + states[0].shape)
    return tuple((arrived[index] for index in range(count_states)))


def expert_gradient(tokens, cotangent, expert_ids, gate_probs, up_weight):
    group_size = lax.axis_size("expert")
    tok_rows, top_count = expert_ids.shape
    width = tokens.shape[1]
    capacity = 3 * tok_rows * top_count // (2 * group_size)
    total = tok_rows * top_count
    flat_ids = expert_ids.reshape(-1)
    picked = (flat_ids[:, None] == jnp.arange(group_size, dtype=jnp.int32)[None, :]).astype(
        jnp.int32
    )
    ranking = jnp.sum((jnp.cumsum(picked, axis=0) - 1) * picked, axis=1)
    slot_index = flat_ids * capacity + ranking
    source = (
        jnp.full((group_size * capacity,), total, jnp.int32)
        .at[slot_index]
        .set(jnp.arange(total, dtype=jnp.int32))
    )
    filled = source < total
    safe_source = jnp.minimum(source, total - 1)
    row_index = safe_source // top_count
    weights_row = jnp.where(filled, gate_probs.reshape(-1)[safe_source], jnp.float32(0.0))
    sent_tokens = jnp.where(filled[:, None], tokens[row_index], jnp.zeros((), jnp.bfloat16))
    sent_scaled = (weights_row[:, None] * cotangent[row_index].astype(jnp.float32)).astype(
        jnp.bfloat16
    )
    sent_tokens = sent_tokens.reshape(group_size, capacity, width)
    sent_scaled = sent_scaled.reshape(group_size, capacity, width)
    got_tokens, got_scaled = (
        lax.all_to_all(sent_tokens, "expert", split_axis=0, concat_axis=0, tiled=True),
        lax.all_to_all(sent_scaled, "expert", split_axis=0, concat_axis=0, tiled=True),
    )
    rows_tokens = got_tokens.reshape(-1, width)
    rows_scaled = got_scaled.reshape(-1, width)
    hidden = jax.nn.silu(
        jnp.dot(
            rows_tokens,
            lax.all_gather(up_weight[0], "dp", axis=1, tiled=True),
            preferred_element_type=jnp.float32,
        )
    ).astype(jnp.bfloat16)
    return lax.psum_scatter(
        lax.dot_general(
            hidden, rows_scaled, (((0,), (0,)), ((), ())), preferred_element_type=jnp.float32
        ),
        "dp",
        scatter_dimension=0,
        tiled=True,
    )


def lamb_step(weight, moment_one, moment_two, gradient):
    first = beta_one * moment_one + (1.0 - beta_one) * gradient
    second = beta_two * moment_two + (1.0 - beta_two) * gradient * gradient
    update = first / (jnp.sqrt(second) + epsilon)
    weight_sq, update_sq = lax.psum((jnp.sum(weight * weight), jnp.sum(update * update)), "dp")
    trust_ratio = jnp.sqrt(weight_sq) / (jnp.sqrt(update_sq) + epsilon)
    renewed = weight - learn_rate * trust_ratio * update
    return (renewed, first, second)


def local(
    tokens, cotangent, expert_ids, gate_probs, up_weight, down_weight, moment1, moment2, pair_match
):
    gradient = expert_gradient(tokens, cotangent, expert_ids, gate_probs, up_weight)
    renewed, first, second = lamb_step(down_weight[0], moment1[0], moment2[0], gradient)
    renewed, first, second = relocate((renewed, first, second), pair_match)
    return (renewed[None], first[None], second[None])


def solution(mesh):
    in_specs = (
        P(("dp", "expert"), None),
        P(("dp", "expert"), None),
        P(("dp", "expert"), None),
        P(("dp", "expert"), None),
        P("expert", None, "dp"),
        P("expert", "dp", None),
        P("expert", "dp", None),
        P("expert", "dp", None),
        P(),
    )
    out_specs = (P("expert", "dp", None), P("expert", "dp", None), P("expert", "dp", None))
    return jax.shard_map(local, mesh=mesh, in_specs=in_specs, out_specs=out_specs, check_vma=False)
```

profile of v0, /device:TPU:1, one launch (start us, length us, event | category | flops | bytes accessed | tf_op | source)
XLA Modules:
  0.0 821.9 jit_solution(15123819818895315411)
XLA Ops:
  7.2 0.0 copy-start
  7.2 0.8 copy.13
  8.0 0.1 eq.29
  8.1 0.1 eq.25
  8.2 0.7 broadcast_multiply_fusion
  8.9 18.0 %reduce-window.6 = s32[64,8,128]{2,1,0:T(8,128)S(1)} reduce-window(s32[64,8,128]{2,1,0:T(8,128)S(1)} %fusion.9, s32[]{:T(128)} %constant.22.clone.1), window={size=1x1x128 pad=0_0x0_0x127_0}, to_apply=%region_2.3 | reduce-window | flops 8323072 | bytes 524292 | tf_op jit(solution)/shard_map/reduce-window
  26.9 0.1 slice.40
  27.1 0.1 copy.15
  27.3 0.1 copy.16
  27.3 0.1 add_add_fusion
  27.5 0.1 copy.12
  27.6 0.1 mul.85
  27.7 0.1 fusion.8
  27.8 4.3 scatter_custom_fusion
  32.1 0.8 copy.17
  32.9 0.1 reshape.103
  33.0 5.9 gather_fusion.1
  38.9 0.1 broadcast_in_dim.42
  39.0 0.0 copy-done
  39.0 7.1 gather_fusion
  46.1 5.9 broadcast_select_fusion
  52.0 0.0 copy-start.2
  52.0 13.3 %all-to-all-start = ((bf16[64,24,2048]{2,1,0:T(8,128)(2,1)}), bf16[64,24,2048]{2,1,0:T(8,128)(2,1)}, u32[]{:S(2)}, u32[]{:S(2)}) async-start(bf16[64,24,2048]{2,1,0:T(8,128)(2,1)} %broadcast_select_fusion), calls=%async_computation | async-start | bytes 12582912 | tf_op jit(solution)/shard_map/all_to_all | solution.py:54
  65.3 0.1 mul.88
  65.4 0.0 copy-done.2
  65.4 7.0 gather_fusion.2
  72.5 6.5 fusion
  78.9 124.9 %all-to-all-done = bf16[64,24,2048]{2,1,0:T(8,128)(2,1)} async-done(((bf16[64,24,2048]{2,1,0:T(8,128)(2,1)}), bf16[64,24,2048]{2,1,0:T(8,128)(2,1)}, u32[]{:S(2)}, u32[]{:S(2)}) %all-to-all-start) | async-done | bytes 6291488 | tf_op jit(solution)/shard_map/all_to_all | solution.py:54
  203.9 8.5 %all-to-all-start.1 = ((bf16[64,24,2048]{2,1,0:T(8,128)(2,1)}), bf16[64,24,2048]{2,1,0:T(8,128)(2,1)}, u32[]{:S(2)}, u32[]{:S(2)}) async-start(bf16[64,24,2048]{2,1,0:T(8,128)(2,1)} %fusion), calls=%async_computation.1 | async-start | bytes 12582912 | tf_op jit(solution)/shard_map/all_to_all | solution.py:55
  212.4 0.0 all-gather.3.cloned.1.call-start
  212.4 0.7 all-gather.3.cloned.1.call-update
  213.1 0.6 reduce-scatter.2.cloned.1.call-start
  213.7 44.6 %all-gather.3.cloned.1.call-done = bf16[1,2048,768]{1,2,0:T(8,128)(2,1)} async-done(((bf16[1,2048,192]{1,2,0:T(8,128)(2,1)}), bf16[1,2048,768]{1,2,0:T(8,128)(2,1)}) %all-gather.3.cloned.1.call-update) | async-done | bytes 3145744 | tf_op jit(solution)/shard_map/all_gather | solution.py:62
  258.3 92.6 %all-to-all-done.1 = bf16[64,24,2048]{2,1,0:T(8,128)(2,1)} async-done(((bf16[64,24,2048]{2,1,0:T(8,128)(2,1)}), bf16[64,24,2048]{2,1,0:T(8,128)(2,1)}, u32[]{:S(2)}, u32[]{:S(2)}) %all-to-all-start.1) | async-done | bytes 6291488 | tf_op jit(solution)/shard_map/all_to_all | solution.py:55
  350.9 27.9 %fusion.15 = f32[768,2048]{1,0:T(8,128)} fusion(bf16[1536,2048]{1,0:T(8,128)(2,1)} %bitcast.10, bf16[1536,2048]{1,0:T(8,128)(2,1)} %bitcast.7, bf16[1,2048,768]{1,2,0:T(8,128)(2,1)} %all-gather.3.cloned.1.call-done), kind=kOutput, calls=%fused_computation.51 | convolution fusion | flops 9669574656 | bytes 22020096 | tf_op jit(solution)/shard_map/dot_general | solution.py:67
  378.8 0.0 copy-start.3
  378.8 0.0 reduce-scatter.2.cloned.1.call-update
  378.8 1.4 copy-done.3
  380.2 1.0 fusion.6
  381.2 63.5 %reduce-scatter.2.cloned.1.call-done = f32[192,2048]{1,0:T(8,128)} async-done(((f32[768,2048]{1,0:T(8,128)}), f32[192,2048]{1,0:T(8,128)}) %reduce-scatter.2.cloned.1.call-update) | async-done | bytes 1572880 | tf_op jit(solution)/shard_map/reduce_scatter | solution.py:66
  444.6 5.0 multiply_reduce_fusion
  449.7 7.2 all-reduce
  458.2 3.0 stack.17
  461.3 3.9 stack.18
  465.3 3.7 bitcast_subtract_fusion
  468.9 0.0 copy-start.4
  468.9 4.1 stack.16
  473.0 0.0 copy-done.4
  473.0 7.3 pad_maximum_fusion
  480.4 0.0 copy-start.5
  480.4 13.3 %all-to-all-start.2 = ((f32[3,64,6144]{2,0,1:T(4,128)}), f32[3,64,6144]{2,0,1:T(4,128)}, u32[]{:S(2)}, u32[]{:S(2)}) async-start(f32[3,64,6144]{2,0,1:T(4,128)} %pad_maximum_fusion), calls=%async_computation.3 | async-start | bytes 12582912 | tf_op jit(solution)/shard_map/all_to_all | solution.py:17
  493.7 0.0 copy-done.5
  493.7 138.5 %all-to-all-done.2 = f32[3,64,6144]{2,0,1:T(4,128)} async-done(((f32[3,64,6144]{2,0,1:T(4,128)}), f32[3,64,6144]{2,0,1:T(4,128)}, u32[]{:S(2)}, u32[]{:S(2)}) %all-to-all-start.2) | async-done | bytes 4718624 | tf_op jit(solution)/shard_map/all_to_all | solution.py:17
  632.2 9.4 %gather_fusion.3 = f32[64,3,6144]{2,1,0:T(4,128)} fusion(f32[3,64,6144]{2,0,1:T(4,128)} %all-to-all-done.2, s32[1024]{0:T(1024)S(1)} %pad_clamp_fusion.2), kind=kCustom, calls=%fused_computation.3 | custom fusion | bytes 9437440 | tf_op jit(solution)/shard_map/jit(_take)/gather | solution.py:16
  641.5 4.5 select_bitcast_fusion
  646.0 147.7 %all_to_all.20 = f32[3,64,6144]{2,0,1:T(4,128)S(1)} all-to-all(f32[3,64,6144]{2,0,1:T(4,128)S(1)} %select_bitcast_fusion), channel_id=1, replica_groups=mesh['dp'=4,'expert'=64] {'expert'}, dimensions={1} | all-to-all | bytes 9437184 | tf_op jit(solution)/shard_map/all_to_all | solution.py:21
  793.8 14.1 %slice_reduce_fusion = (f32[64,6144]{1,0:T(8,128)S(1)}, f32[64,6144]{1,0:T(8,128)}, f32[64,6144]{1,0:T(8,128)}) fusion(f32[3,64,6144]{2,0,1:T(4,128)S(1)} %all_to_all.20), kind=kLoop, calls=%fused_computation.15 | loop fusion | bytes 9437184 | tf_op jit(solution)/shard_map/slice | solution.py:23
  807.9 2.7 slice.27
  810.6 0.0 copy-start.1
  810.6 2.7 slice.29
  813.3 1.5 slice.31
  814.8 0.0 copy-done.1
  (11 shorter events, 0.1 us)
Async XLA Ops:
  7.2 31.8 %copy-start = (bf16[128,2048]{1,0:T(8,128)(2,1)S(1)}, bf16[128,2048]{1,0:T(8,128)(2,1)}, u32[]{:S(2)}) copy-start(bf16[128,2048]{1,0:T(8,128)(2,1)} %param.9) | copy-start | bytes 1572868
  52.0 13.4 %copy-start.2 = (bf16[128,2048]{1,0:T(8,128)(2,1)S(1)}, bf16[128,2048]{1,0:T(8,128)(2,1)}, u32[]{:S(2)}) copy-start(bf16[128,2048]{1,0:T(8,128)(2,1)} %param.10) | copy-start | bytes 1572868
  52.0 151.8 %all-to-all-start = ((bf16[64,24,2048]{2,1,0:T(8,128)(2,1)}), bf16[64,24,2048]{2,1,0:T(8,128)(2,1)}, u32[]{:S(2)}, u32[]{:S(2)}) async-start(bf16[64,24,2048]{2,1,0:T(8,128)(2,1)} %broadcast_select_fusion), calls=%async_computation | async-start | bytes 12582912 | tf_op jit(solution)/shard_map/all_to_all | solution.py:54
  203.9 147.0 %all-to-all-start.1 = ((bf16[64,24,2048]{2,1,0:T(8,128)(2,1)}), bf16[64,24,2048]{2,1,0:T(8,128)(2,1)}, u32[]{:S(2)}, u32[]{:S(2)}) async-start(bf16[64,24,2048]{2,1,0:T(8,128)(2,1)} %fusion), calls=%async_computation.1 | async-start | bytes 12582912 | tf_op jit(solution)/shard_map/all_to_all | solution.py:55
  212.4 45.9 %all-gather.3.cloned.1.call-start = ((), (), s32[]{:S(2)}) async-start(), calls=%async_computation.6 | async-start | bytes 3932160 | tf_op jit(solution)/shard_map/all_gather | solution.py:62
  213.1 231.5 %reduce-scatter.2.cloned.1.call-start = ((), (), s32[]{:S(2)}) async-start(), calls=%async_computation.5 | async-start | bytes 7864320 | tf_op jit(solution)/shard_map/reduce_scatter | solution.py:66
  378.8 1.4 copy-start.3
  468.9 4.1 copy-start.4
  480.4 13.3 %copy-start.5 = (s32[64]{0:T(128)S(1)}, s32[64]{0:T(128)}, u32[]{:S(2)}) copy-start(s32[64]{0:T(128)} %param.17) | copy-start | bytes 772
  480.4 151.8 %all-to-all-start.2 = ((f32[3,64,6144]{2,0,1:T(4,128)}), f32[3,64,6144]{2,0,1:T(4,128)}, u32[]{:S(2)}, u32[]{:S(2)}) async-start(f32[3,64,6144]{2,0,1:T(4,128)} %pad_maximum_fusion), calls=%async_computation.3 | async-start | bytes 12582912 | tf_op jit(solution)/shard_map/all_to_all | solution.py:17
  810.6 4.2 copy-start.1
Sparse Core Ops, SparseCore 0:
  215.0 43.2 all-gather.2
  378.9 65.6 reduce-scatter.1
where the time goes:
time: 829 us; the launch traced here: 822 us
  waiting for transfers between devices  465 us (56%)
  blocking collectives  155 us (19%)
  local copies, waits for them, and re-layouts  69.8 us (8%)
  other arithmetic  53 us (6%)
  starting transfers between devices  35.7 us (4%)
  matrix products  27.9 us (3%)
  between operations  15.9 us (2%)
    all_to_all x1, blocking collectives, relocate(): lax.all_to_all(chosen, 'expert', split_axis=1, concat_axis=1, tiled=True)  148 us
    all_to_all x1, waiting for transfers between devices, relocate(): lax.all_to_all(stacked, 'expert', split_axis=1, concat_axis=1, tiled=True)  138 us
    all_to_all x1, waiting for transfers between devices, expert_gradient(): lax.all_to_all(sent_tokens, 'expert', split_axis=0, concat_axis=0, tiled=...  125 us
    all_to_all x1, waiting for transfers between devices, expert_gradient(): lax.all_to_all(sent_scaled, 'expert', split_axis=0, concat_axis=0, tiled=...  92.6 us
    reduce_scatter x1, waiting for transfers between devices, expert_gradient(): lax.psum_scatter(lax.dot_general(hidden, rows_scaled, (((0,), (0,)), ((),...  63.5 us
    all_gather x1, waiting for transfers between devices, expert_gradient(): lax.all_gather(up_weight[0], 'dp', axis=1, tiled=True)  44.6 us
    dot_general x1, matrix products, expert_gradient(): lax.dot_general(hidden, rows_scaled, (((0,), (0,)), ((), ())), preferred_...  27.9 us
    slice x4, local copies, waits for them, and re-layouts, relocate(): return tuple((arrived[index] for index in range(count_states)))  21 us
  transfers between devices with their start and end apart: 5, of which 5 were waited for; matrix products, arithmetic and copies ran while one was open for 2% of the time, Pallas kernels for 0%

commit v1 on v0

v1 whole, which is shorter than its diff:
```python
import functools

import jax
import jax.numpy as jnp
from jax import lax
from jax.experimental import pallas as pl
from jax.experimental.pallas import tpu as pltpu
from jax.sharding import PartitionSpec as P

beta_one = 0.9
beta_two = 0.999
epsilon = 1e-06
learn_rate = 0.05

NZ = 8
PLANE = 8
NY = 4
CAP = 24
TOK = 128
PAIRS = NZ // 2
CHUNKS = 4
MESH = pl.DeviceIdType.MESH


def gradient_kernel(
    tok, cot, meta, up, out,
    zt, zc, zm, sel, prob, sbt, sbs, rbt, rbs, upb, hid, gbuf, grecv,
    zt_s, zt_r, zm_s, zm_r, zc_s, zc_r, up_s, up_r, xt_s, xt_r, xc_s, xc_r, g_s, g_r, loc,
):
    f32, bf16 = jnp.float32, jnp.bfloat16
    width = tok.shape[1]
    chunk = width // CHUNKS
    slice_rows = up.shape[0]
    y = lax.axis_index("dp")
    e = lax.axis_index("expert")
    total = NZ * PLANE
    z = e // PLANE
    p = lax.rem(e, PLANE)
    right = (y, lax.rem(e + PLANE, total))
    left = (y, lax.rem(e + total - PLANE, total))

    def mate(o):
        q = lax.rem(p + o, PLANE)
        return q, (y, z * PLANE + q)

    def layer(o):
        k = lax.rem(y + o, NY)
        return k, (k, e)

    barrier = pltpu.get_barrier_semaphore()
    partners = [right, left]
    partners += [mate(o)[1] for o in range(1, PLANE)]
    partners += [layer(o)[1] for o in range(1, NY)]
    for partner in partners:
        pl.semaphore_signal(barrier, inc=1, device_id=partner, device_id_type=MESH)
    pl.semaphore_wait(barrier, len(partners))

    def remote(src, dst, send, recv, device):
        return pltpu.make_async_remote_copy(
            src_ref=src, dst_ref=dst, send_sem=send, recv_sem=recv,
            device_id=device, device_id_type=MESH,
        )

    def held(direction, step):
        return 0 if step == 1 else 2 * (step - 1) + direction

    def landing(direction, step):
        return 1 if step == 4 else 2 * step + direction

    half = TOK // 2

    def z_copy(ring, send, recv, direction, step):
        src, dst = ring.at[held(direction, step)], ring.at[landing(direction, step)]
        if step == 4:
            rows = pl.ds(direction * half, half)
            src, dst = src.at[rows], dst.at[rows]
        return remote(src, dst, send.at[direction, step], recv.at[direction, step],
                      left if direction else right)

    def tok_copy(direction, step):
        return z_copy(zt, zt_s, zt_r, direction, step)

    def cot_copy(c, direction, step):
        return z_copy(zc.at[c], zc_s.at[c], zc_r.at[c], direction, step)

    def meta_copy(direction, step):
        return remote(zm.at[held(direction, step)], zm.at[landing(direction, step)],
                      zm_s.at[direction, step], zm_r.at[direction, step],
                      left if direction else right)

    def meta_steps(step):
        return (0,) if step == 4 else (0, 1)

    zm[0] = meta[...]
    zt[0] = tok[...]
    for c in range(CHUNKS):
        zc[c, 0] = cot[:, c * chunk:(c + 1) * chunk]

    for d in (0, 1):
        meta_copy(d, 1).start()
        tok_copy(d, 1).start()

    own_up = pltpu.make_async_copy(up, upb.at[y], loc.at[0])
    own_up.start()

    def up_copy(o):
        k, device = layer(o)
        return remote(up, upb.at[y], up_s.at[o], up_r.at[o], device)

    for o in (2, 1, 3):
        up_copy(o).start()

    for c in range(CHUNKS):
        for d in (0, 1):
            cot_copy(c, d, 1).start()

    row_of = lax.broadcasted_iota(jnp.int32, (TOK, TOK), 0)
    col_of = lax.broadcasted_iota(jnp.int32, (TOK, TOK), 1)
    before = (row_of < col_of).astype(f32).astype(bf16)
    first_expert = (z * PLANE).astype(f32)
    expert_of = lax.broadcasted_iota(jnp.int32, (PLANE, TOK), 0).astype(f32) + first_expert
    place_of = lax.broadcasted_iota(jnp.int32, (PLANE, CAP, TOK), 1).astype(f32)

    def select_of(slot):
        mask = jnp.zeros((PLANE, TOK), f32)
        weight = jnp.zeros((PLANE, TOK), f32)
        top = meta.shape[0] // 2
        for k in range(top):
            hit = zm[slot, k:k + 1, :] == expert_of
            mask = jnp.where(hit, 1.0, mask)
            weight = jnp.where(hit, zm[slot, top + k:top + k + 1, :], weight)
        rank = jnp.dot(mask.astype(bf16), before, preferred_element_type=f32)
        rank = jnp.where(mask > 0.5, rank, -1.0)
        picked = jnp.where(rank[:, None, :] == place_of, 1.0, 0.0)
        gate = jnp.sum(picked * weight[:, None, :], axis=2, keepdims=True)
        return picked, gate

    def build(j):
        first_pick, first_gate = select_of(2 * j)
        second_pick, second_gate = select_of(2 * j + 1)
        blank = jnp.zeros((PLANE, CAP, TOK), f32)
        both = jnp.concatenate(
            [jnp.concatenate([first_pick, blank], axis=2),
             jnp.concatenate([blank, second_pick], axis=2)], axis=1)
        sel[j] = both.reshape(PLANE * 2 * CAP, 2 * TOK).astype(bf16)
        prob[j] = jnp.concatenate([first_gate, second_gate], axis=1).reshape(PLANE * 2 * CAP, 1)

    def xt_copy(j, o):
        q, device = mate(o)
        return remote(sbt.at[j, q], rbt.at[p, j], xt_s.at[j, o], xt_r.at[j, o], device)

    def xt_own(j):
        return pltpu.make_async_copy(sbt.at[j, p], rbt.at[p, j], loc.at[1 + j])

    def xc_copy(c, o):
        q, device = mate(o)
        return remote(sbs.at[c, q], rbs.at[c, p], xc_s.at[c, o], xc_r.at[c, o], device)

    def xc_own(c):
        return pltpu.make_async_copy(sbs.at[c, p], rbs.at[c, p], loc.at[1 + PAIRS + c])

    order = (4, 2, 6, 3, 5, 1, 7)

    def send_tokens(j):
        build(j)

        @pl.loop(0, CHUNKS)
        def _(c):
            cols = pl.ds(pl.multiple_of(c * chunk, chunk), chunk)
            pair = zt[2 * j:2 * j + 2, :, cols].reshape(2 * TOK, chunk)
            rows = jnp.dot(sel[j], pair, preferred_element_type=f32)
            sbt[j, :, :, cols] = rows.astype(bf16).reshape(PLANE, 2 * CAP, chunk)

        xt_own(j).start()
        for o in order:
            xt_copy(j, o).start()

    for step in (1, 2, 3, 4):
        for d in (0, 1):
            if d in meta_steps(step):
                meta_copy(d, step).wait_recv()
                if step < 4 and d in meta_steps(step + 1):
                    meta_copy(d, step + 1).start()
            tok_copy(d, step).wait_recv()
            if step < 4:
                tok_copy(d, step + 1).start()
        send_tokens(0 if step == 4 else step)

    for step in (1, 2, 3, 4):
        for c in range(CHUNKS):
            for d in (0, 1):
                cot_copy(c, d, step).wait_recv()
                if step < 4:
                    cot_copy(c, d, step + 1).start()
            if step == 4:
                for j in range(PAIRS):
                    pair = zc[c, 2 * j:2 * j + 2].reshape(2 * TOK, chunk)
                    rows = jnp.dot(sel[j], pair, preferred_element_type=f32) * prob[j]
                    sbs[c, :, j] = rows.astype(bf16).reshape(PLANE, 2 * CAP, chunk)
                xc_own(c).start()
                for o in order:
                    xc_copy(c, o).start()

    own_up.wait()
    for o in range(1, NY):
        up_copy(o).wait_recv()
    for j in range(PAIRS):
        xt_own(j).wait()
        for o in range(1, PLANE):
            xt_copy(j, o).wait_recv()
    span = 2 * PAIRS * 2 * CAP

    @pl.loop(0, PLANE // 2)
    def _(m):
        rows = rbt[pl.ds(2 * m, 2)].reshape(span, width)
        cols = pl.ds(pl.multiple_of(m * span, span), span)

        @pl.loop(0, NY)
        def _(k):
            v = lax.dot_general(upb[k], rows, (((1,), (1,)), ((), ())), preferred_element_type=f32)
            units = pl.ds(pl.multiple_of(k * slice_rows, slice_rows), slice_rows)
            hid[units, cols] = (v / (1.0 + jnp.exp(-v))).astype(bf16)

    def g_copy(c, o):
        k, device = layer(o)
        return remote(gbuf.at[c, k], grecv.at[c, o - 1], g_s.at[c, o], g_r.at[c, o], device)

    for c in range(CHUNKS):
        xc_own(c).wait()
        for o in range(1, PLANE):
            xc_copy(c, o).wait_recv()

        @pl.loop(0, NY)
        def _(k):
            units = pl.ds(pl.multiple_of(k * slice_rows, slice_rows), slice_rows)
            rows = rbs[c].reshape(PLANE * PAIRS * 2 * CAP, chunk)
            gbuf[c, k] = jnp.dot(hid[units, :], rows, preferred_element_type=f32)

        for o in (2, 1, 3):
            g_copy(c, o).start()

    for c in range(CHUNKS):
        for o in range(1, NY):
            g_copy(c, o).wait_recv()
        summed = (gbuf[c, y] + grecv[c, 0]) + (grecv[c, 1] + grecv[c, 2])
        out[:, c * chunk:(c + 1) * chunk] = summed

    for step in (1, 2, 3, 4):
        for d in (0, 1):
            if d in meta_steps(step):
                meta_copy(d, step).wait_send()
            tok_copy(d, step).wait_send()
            for c in range(CHUNKS):
                cot_copy(c, d, step).wait_send()
    for o in range(1, NY):
        up_copy(o).wait_send()
        for c in range(CHUNKS):
            g_copy(c, o).wait_send()
    for o in range(1, PLANE):
        for j in range(PAIRS):
            xt_copy(j, o).wait_send()
        for c in range(CHUNKS):
            xc_copy(c, o).wait_send()


def expert_gradient(tokens, cotangent, expert_ids, gate_probs, up_weight):
    rows, width = tokens.shape
    chunk = width // CHUNKS
    units = up_weight.shape[2]
    bf16, f32 = jnp.bfloat16, jnp.float32
    meta = jnp.concatenate([expert_ids.astype(f32).T, gate_probs.T], axis=0)
    up = up_weight[0].T
    pick = PLANE * 2 * CAP
    dma = pltpu.SemaphoreType.DMA
    return pl.pallas_call(
        gradient_kernel,
        out_shape=jax.ShapeDtypeStruct((units, width), f32),
        in_specs=[pl.BlockSpec(memory_space=pltpu.VMEM)] * 4,
        out_specs=pl.BlockSpec(memory_space=pltpu.VMEM),
        scratch_shapes=[
            pltpu.VMEM((NZ, rows, width), bf16),
            pltpu.VMEM((CHUNKS, NZ, rows, chunk), bf16),
            pltpu.VMEM((NZ,) + meta.shape, f32),
            pltpu.VMEM((PAIRS, pick, 2 * rows), bf16),
            pltpu.VMEM((PAIRS, pick, 1), f32),
            pltpu.VMEM((PAIRS, PLANE, 2 * CAP, width), bf16),
            pltpu.VMEM((CHUNKS, PLANE, PAIRS, 2 * CAP, chunk), bf16),
            pltpu.VMEM((PLANE, PAIRS, 2 * CAP, width), bf16),
            pltpu.VMEM((CHUNKS, PLANE, PAIRS, 2 * CAP, chunk), bf16),
            pltpu.VMEM((NY, units, width), bf16),
            pltpu.VMEM((NY * units, PAIRS * pick), bf16),
            pltpu.VMEM((CHUNKS, NY, units, chunk), f32),
            pltpu.VMEM((CHUNKS, NY - 1, units, chunk), f32),
            dma((2, 5)), dma((2, 5)),
            dma((2, 5)), dma((2, 5)),
            dma((CHUNKS, 2, 5)), dma((CHUNKS, 2, 5)),
            dma((NY,)), dma((NY,)),
            dma((PAIRS, PLANE)), dma((PAIRS, PLANE)),
            dma((CHUNKS, PLANE)), dma((CHUNKS, PLANE)),
            dma((CHUNKS, NY)), dma((CHUNKS, NY)),
            dma((1 + PAIRS + CHUNKS,)),
        ],
        compiler_params=pltpu.CompilerParams(
            collective_id=0, has_side_effects=True, vmem_limit_bytes=62 * 2**20
        ),
        cost_estimate=pl.CostEstimate(
            flops=4 * PAIRS * pick * width * units * NY,
            bytes_accessed=4 * rows * width + 2 * units * width * 3,
            transcendentals=PAIRS * pick * units * NY,
        ),
    )(tokens, cotangent, meta, up)


def pick_kernel(match, src, out):
    @pl.loop(0, src.shape[0])
    def _(i):
        out[i] = src[match[i]]


def relocate(states, pair_match):
    group_size = lax.axis_size("expert")
    count = len(states)
    rows, width = states[0].shape
    high, lanes = rows // 4, 128
    across = width // lanes
    pieces = [s.reshape(4, high, across, lanes).transpose(0, 2, 1, 3) for s in states]
    stacked = jnp.stack(pieces, axis=2).reshape(group_size, count * high, lanes)
    spread = lax.all_to_all(stacked, "expert", split_axis=0, concat_axis=0, tiled=True)
    chosen = pl.pallas_call(
        pick_kernel,
        out_shape=jax.ShapeDtypeStruct(spread.shape, spread.dtype),
        in_specs=[pl.BlockSpec(memory_space=pltpu.SMEM), pl.BlockSpec(memory_space=pltpu.VMEM)],
        out_specs=pl.BlockSpec(memory_space=pltpu.VMEM),
        compiler_params=pltpu.CompilerParams(vmem_limit_bytes=32 * 2**20),
    )(pair_match, spread)
    arrived = lax.all_to_all(chosen, "expert", split_axis=0, concat_axis=0, tiled=True)
    arrived = arrived.reshape(4, across, count, high, lanes).transpose(2, 0, 3, 1, 4)
    arrived = arrived.reshape(count, rows, width)
    return tuple(arrived[i] for i in range(count))


def lamb_step(weight, moment_one, moment_two, gradient):
    first = beta_one * moment_one + (1.0 - beta_one) * gradient
    second = beta_two * moment_two + (1.0 - beta_two) * gradient * gradient
    update = first / (jnp.sqrt(second) + epsilon)
    weight_sq, update_sq = lax.psum((jnp.sum(weight * weight), jnp.sum(update * update)), "dp")
    trust_ratio = jnp.sqrt(weight_sq) / (jnp.sqrt(update_sq) + epsilon)
    renewed = weight - learn_rate * trust_ratio * update
    return (renewed, first, second)


def local(
    tokens, cotangent, expert_ids, gate_probs, up_weight, down_weight, moment1, moment2, pair_match
):
    gradient = expert_gradient(tokens, cotangent, expert_ids, gate_probs, up_weight)
    renewed, first, second = lamb_step(down_weight[0], moment1[0], moment2[0], gradient)
    renewed, first, second = relocate((renewed, first, second), pair_match)
    return (renewed[None], first[None], second[None])


def solution(mesh):
    in_specs = (
        P(("dp", "expert"), None),
        P(("dp", "expert"), None),
        P(("dp", "expert"), None),
        P(("dp", "expert"), None),
        P("expert", None, "dp"),
        P("expert", "dp", None),
        P("expert", "dp", None),
        P("expert", "dp", None),
        P(),
    )
    out_specs = (P("expert", "dp", None), P("expert", "dp", None), P("expert", "dp", None))
    return jax.shard_map(local, mesh=mesh, in_specs=in_specs, out_specs=out_specs, check_vma=False)
```

time: 829 us -> 460 us (0.55)
  waiting for transfers between devices: 465 us -> 0 us
  Pallas kernels: 0 us -> 195 us
  blocking collectives: 155 us -> 238 us
  local copies, waits for them, and re-layouts: 69.8 us -> 14.8 us
  other arithmetic: 53 us -> 10.1 us
  starting transfers between devices: 35.7 us -> 0 us
  matrix products: 27.9 us -> 0 us
  between operations: 15.9 us -> 2.12 us
    all_to_all x3 -> x0, waiting for transfers between devices: 356 us -> none  [the longest x1 138 us: relocate(): lax.all_to_all(stacked, 'expert', split_axis=1, concat_axis=1, tiled=True)]
    pallas_call x0 -> x2, Pallas kernels: none -> 195 us  [the longest x1 194 us: expert_gradient(): pl.pallas_call(gradient_kernel, out_shape=jax.ShapeDtypeStruct((units, wi...]
    all_to_all x1 -> x2, blocking collectives: 148 us -> 230 us  [the longest x1 117 us: relocate(): lax.all_to_all(stacked, 'expert', split_axis=0, concat_axis=0, tiled=True)]
    reduce_scatter x1 -> x0, waiting for transfers between devices: 63.5 us -> none  [expert_gradient(): lax.psum_scatter(lax.dot_general(hidden, rows_scaled, (((0,), (0,)), ((),...]
    all_gather x1 -> x0, waiting for transfers between devices: 44.6 us -> none  [expert_gradient(): lax.all_gather(up_weight[0], 'dp', axis=1, tiled=True)]
    all_to_all x3 -> x0, starting transfers between devices: 35.1 us -> none  [the longest x1 13.3 us: relocate(): lax.all_to_all(stacked, 'expert', split_axis=1, concat_axis=1, tiled=True)]
    gather x4 -> x0, local copies, waits for them, and re-layouts: 29.3 us -> none  [the longest x1 9.35 us: relocate(): jnp.take(lax.all_to_all(stacked, 'expert', split_axis=1, concat_axis=1, t...]
    dot_general x1 -> x0, matrix products: 27.9 us -> none  [expert_gradient(): lax.dot_general(hidden, rows_scaled, (((0,), (0,)), ((), ())), preferred_...]
  transfers between devices with their start and end apart: 5 -> 0, of which waited for: 5 -> 0; matrix products, arithmetic and copies ran while one was open for 2% -> 0% of each run, Pallas kernels for 0% -> 0%
where the time goes in v1:
time: 460 us
  blocking collectives  238 us (52%)
  Pallas kernels  195 us (42%)
  local copies, waits for them, and re-layouts  14.8 us (3%)
  other arithmetic  10.1 us (2%)
    pallas_call x1, Pallas kernels, expert_gradient(): pl.pallas_call(gradient_kernel, out_shape=jax.ShapeDtypeStruct((units, wi...  194 us
    all_to_all x1, blocking collectives, relocate(): lax.all_to_all(stacked, 'expert', split_axis=0, concat_axis=0, tiled=True)  117 us
    all_to_all x1, blocking collectives, relocate(): lax.all_to_all(chosen, 'expert', split_axis=0, concat_axis=0, tiled=True)  113 us
    slice x7, local copies, waits for them, and re-layouts, relocate(): return tuple((arrived[i] for i in range(count)))  10.6 us

profile of v1, /device:TPU:1, one launch (start us, length us, event | category | flops | bytes accessed | tf_op | source)
XLA Modules:
  0.0 459.7 jit_solution(7037786256451556660)
XLA Ops:
  0.6 0.7 convert_bitcast_fusion
  1.3 1.3 pad_maximum_fusion.1.meta
  2.6 0.0 copy-start.1
  2.6 193.9 %shard_map.112 = f32[192,2048]{1,0:T(8,128)} custom-call(bf16[128,2048]{1,0:T(8,128)(2,1)} %tok.1, bf16[128,2048]{1,0:T(8,128)(2,1)} %cot.1, f32[16,128]{1,0:T(8,128)} %pad_maximum_fusion.1.meta, bf16[192,2048]{1,0:T(8,128)(2,1)} %bitcast.73), custom_call_target="tpu_custom_call" | custom-call | flops 9663676416 | bytes 3407872 | tf_op jit(solution)/shard_map/pallas_call | solution.py:275
  196.6 0.0 copy-done.1
  196.6 6.1 %multiply_reduce_fusion = (f32[]{:T(128)}, f32[192,2048]{1,0:T(8,128)}, f32[24,8,16,128]{3,1,2,0:T(8,128)}, f32[24,8,16,128]{3,1,2,0:T(8,128)}, f32[]{:T(128)}) fusion(f32[192,2048]{1,0:T(8,128)} %shard_map.112, f32[1,192,2048]{2,1,0:T(8,128)} %param.16, f32[1,192,2048]{2,1,0:T(8,128)} %param.15, f32[1,192,2048]{2,1,0:T(8,128)S(1)} %copy-done.1), kind=kLoop, calls=%fused_computation.11 | loop fusion | flops 5111806 | bytes 11010056 | tf_op jit(solution)/shard_map/reduce_sum | solution.py:346
  202.7 7.2 %all-reduce = (f32[]{:T(128)}, f32[]{:T(128)}) all-reduce(f32[]{:T(128)} %get-tuple-element.12, f32[]{:T(128)} %get-tuple-element.5), channel_id=1, replica_groups=mesh['dp'=4,'expert'=64] {'dp'}, use_global_device_ids=true, to_apply=%region_1.0 | all-reduce | flops 2 | bytes 16 | tf_op jit(solution)/shard_map/psum | solution.py:346
  211.2 1.6 fusion.2
  212.8 0.3 copy.18
  213.1 0.0 copy-start.3
  213.1 0.5 copy.26
  213.6 0.9 copy-done.3
  214.5 0.3 copy.19
  214.8 0.0 copy-start.2
  214.8 0.5 copy.25
  215.3 0.9 copy-done.2
  216.2 0.3 copy.20
  216.5 0.5 copy.24
  217.0 0.4 pad_maximum_fusion
  217.4 0.0 copy-start
  217.4 117.3 %all_to_all.10.src = f32[64,144,128]{2,1,0:T(8,128)S(1)} all-to-all(f32[64,144,128]{2,1,0:T(8,128)S(1)} %bitcast.65), channel_id=1, replica_groups=mesh['dp'=4,'expert'=64] {'expert'}, dimensions={0} | all-to-all | bytes 9437184 | tf_op jit(solution)/shard_map/all_to_all | solution.py:328
  334.7 0.0 copy-done
  334.7 1.2 shard_map.113
  335.9 113.1 %all_to_all.11 = f32[64,144,128]{2,1,0:T(8,128)S(1)} all-to-all(f32[64,144,128]{2,1,0:T(8,128)S(1)} %shard_map.113), channel_id=1, replica_groups=mesh['dp'=4,'expert'=64] {'expert'}, dimensions={0} | all-to-all | bytes 9437184 | tf_op jit(solution)/shard_map/all_to_all | solution.py:336
  449.0 0.5 fusion.5
  449.5 1.6 copy.17
  451.1 2.5 slice.23
  453.7 1.6 copy.16
  455.3 2.5 slice.21
  457.8 0.5 copy.15
  458.3 1.4 slice.19
Async XLA Ops:
  2.6 193.9 %copy-start.1 = (f32[1,192,2048]{2,1,0:T(8,128)S(1)}, f32[1,192,2048]{2,1,0:T(8,128)}, u32[]{:S(2)}) copy-start(f32[1,192,2048]{2,1,0:T(8,128)} %param.14) | copy-start | bytes 4718596
  213.1 1.4 copy-start.3
  214.8 1.4 copy-start.2
  217.4 117.4 %copy-start = (s32[64]{0:T(128)S(1)}, s32[64]{0:T(128)}, u32[]{:S(2)}) copy-start(s32[64]{0:T(128)} %match.1) | copy-start | bytes 772

commit v2 on v1

--- a/solution.py
+++ b/solution.py
@@ -1,5 +1,3 @@
-import functools
-
 import jax
 import jax.numpy as jnp
 from jax import lax
@@ -19,25 +17,36 @@
 TOK = 128
 PAIRS = NZ // 2
 CHUNKS = 4
+VMEM_BYTES = 62 * 2**20
+TOTAL = NZ * PLANE
+HIGH, LANES = 48, 128
+ACROSS = 16
+WORDS = HIGH // 2
+STATES = 3
+STEP = 0.6931471805599453 / 8.0
+LEVELS = 32767.0
 MESH = pl.DeviceIdType.MESH
 
 
-def gradient_kernel(
-    tok, cot, meta, up, out,
+def step_kernel(
+    match, meta, tok, cot, up, weight, moment1, moment2, new_w, new_1, new_2,
     zt, zc, zm, sel, prob, sbt, sbs, rbt, rbs, upb, hid, gbuf, grecv,
-    zt_s, zt_r, zm_s, zm_r, zc_s, zc_r, up_s, up_r, xt_s, xt_r, xc_s, xc_r, g_s, g_r, loc,
+    stg, mid, fin, upmid, upout, norm, norm_in,
+    zt_s, zt_r, zm_s, zm_r, zc_s, zc_r, up_s, up_r, xt_s, xt_r, xc_s, xc_r, g_s, g_r, n_s, n_r,
+    ex_s, ex_r, loc, load, store,
 ):
-    f32, bf16 = jnp.float32, jnp.bfloat16
+    f32, bf16, i32 = jnp.float32, jnp.bfloat16, jnp.int32
     width = tok.shape[1]
     chunk = width // CHUNKS
+    per_chunk = chunk // LANES
     slice_rows = up.shape[0]
+    groups = slice_rows // HIGH
     y = lax.axis_index("dp")
     e = lax.axis_index("expert")
-    total = NZ * PLANE
     z = e // PLANE
     p = lax.rem(e, PLANE)
-    right = (y, lax.rem(e + PLANE, total))
-    left = (y, lax.rem(e + total - PLANE, total))
+    right = (y, lax.rem(e + PLANE, TOTAL))
+    left = (y, lax.rem(e + TOTAL - PLANE, TOTAL))
 
     def mate(o):
         q = lax.rem(p + o, PLANE)
@@ -47,13 +56,31 @@
         k = lax.rem(y + o, NY)
         return k, (k, e)
 
+    tok_load = pltpu.make_async_copy(tok, zt.at[0], load.at[0])
+    tok_load.start()
+    cot_loads = [
+        pltpu.make_async_copy(cot.at[:, pl.ds(c * chunk, chunk)], zc.at[c, 0], load.at[1 + c])
+        for c in range(CHUNKS)
+    ]
+    state_loads = [
+        pltpu.make_async_copy(
+            ref.at[:, pl.ds(c * chunk, chunk)], gbuf.at[a, c], load.at[1 + CHUNKS + a * CHUNKS + c])
+        for a, ref in enumerate((weight, moment1, moment2)) for c in range(CHUNKS)
+    ]
+    for copy in state_loads + cot_loads:
+        copy.start()
+    zm[0] = meta[...]
+
     barrier = pltpu.get_barrier_semaphore()
-    partners = [right, left]
-    partners += [mate(o)[1] for o in range(1, PLANE)]
-    partners += [layer(o)[1] for o in range(1, NY)]
-    for partner in partners:
-        pl.semaphore_signal(barrier, inc=1, device_id=partner, device_id_type=MESH)
-    pl.semaphore_wait(barrier, len(partners))
+
+    @pl.loop(1, TOTAL)
+    def _(o):
+        pl.semaphore_signal(
+            barrier, inc=1, device_id=(y, lax.rem(e + o, TOTAL)), device_id_type=MESH)
+
+    for o in range(1, NY):
+        pl.semaphore_signal(barrier, inc=1, device_id=layer(o)[1], device_id_type=MESH)
+    pl.semaphore_wait(barrier, TOTAL - 1 + NY - 1)
 
     def remote(src, dst, send, recv, device):
         return pltpu.make_async_remote_copy(
@@ -91,48 +118,83 @@
     def meta_steps(step):
         return (0,) if step == 4 else (0, 1)
 
-    zm[0] = meta[...]
-    zt[0] = tok[...]
-    for c in range(CHUNKS):
-        zc[c, 0] = cot[:, c * chunk:(c + 1) * chunk]
-
+    tok_load.wait()
     for d in (0, 1):
         meta_copy(d, 1).start()
         tok_copy(d, 1).start()
 
-    own_up = pltpu.make_async_copy(up, upb.at[y], loc.at[0])
+    def piece_of(q):
+        rows = pl.ds(pl.multiple_of((q // ACROSS) * HIGH, HIGH), HIGH)
+        cols = pl.ds(pl.multiple_of(lax.rem(q, ACROSS) * LANES, LANES), LANES)
+        return rows, cols
+
+    def all_pieces(buffer, index):
+        span = pl.ds(0, TOTAL - 1)
+        return remote(buffer.at[span], buffer.at[span], ex_s.at[index], ex_r.at[index], right)
+
+    @pl.loop(1, TOTAL)
+    def _(o):
+        q = lax.rem(e + o, TOTAL)
+        rows, cols = piece_of(q)
+        remote(up.at[rows, cols], upmid.at[e], ex_s.at[0], ex_r.at[0], (y, q)).start()
+
+    own_rows, own_cols = piece_of(e)
+    own_up = pltpu.make_async_copy(up.at[own_rows, own_cols], upmid.at[e], loc.at[0])
     own_up.start()
+
+    scale_row = lax.broadcasted_iota(i32, (8, LANES), 0)
+    for copy in state_loads:
+        copy.wait()
+
+    @pl.loop(0, CHUNKS)
+    def _(c):
+        for h in range(per_chunk):
+            for g in range(groups):
+                q = g * ACROSS + c * per_chunk + h
+                powers = jnp.zeros((8, LANES), f32)
+                for a in range(STATES):
+                    x = gbuf[a, c, g * HIGH:(g + 1) * HIGH, h * LANES:(h + 1) * LANES]
+                    most = jnp.maximum(jnp.max(jnp.abs(x), axis=0, keepdims=True), 1e-30)
+                    power = jnp.ceil(jnp.log(most) * (1.0 / STEP))
+                    inverse = 1.0 / (jnp.exp(power * STEP) * (1.0 / LEVELS))
+                    code = jnp.clip(jnp.floor(x * inverse + 0.5), -LEVELS, LEVELS).astype(i32)
+                    stg[q, a * WORDS:(a + 1) * WORDS] = code[:WORDS] * 65536 + (code[WORDS:] + 32768)
+                    powers = jnp.where(scale_row == a, power, powers)
+                stg[q, STATES * WORDS:] = powers.astype(i32)
+
+    @pl.loop(1, TOTAL)
+    def _(o):
+        q = lax.rem(e + o, TOTAL)
+        remote(stg.at[q], mid.at[e], ex_s.at[1], ex_r.at[1], (y, q)).start()
+
+    mid[e] = stg[e]
 
     def up_copy(o):
         k, device = layer(o)
-        return remote(up, upb.at[y], up_s.at[o], up_r.at[o], device)
-
-    for o in (2, 1, 3):
-        up_copy(o).start()
-
-    for c in range(CHUNKS):
-        for d in (0, 1):
-            cot_copy(c, d, 1).start()
-
-    row_of = lax.broadcasted_iota(jnp.int32, (TOK, TOK), 0)
-    col_of = lax.broadcasted_iota(jnp.int32, (TOK, TOK), 1)
+        return remote(upb.at[y], upb.at[y], up_s.at[o], up_r.at[o], device)
+
+    row_of = lax.broadcasted_iota(i32, (TOK, TOK), 0)
+    col_of = lax.broadcasted_iota(i32, (TOK, TOK), 1)
     before = (row_of < col_of).astype(f32).astype(bf16)
-    first_expert = (z * PLANE).astype(f32)
-    expert_of = lax.broadcasted_iota(jnp.int32, (PLANE, TOK), 0).astype(f32) + first_expert
-    place_of = lax.broadcasted_iota(jnp.int32, (PLANE, CAP, TOK), 1).astype(f32)
+    place_of = lax.broadcasted_iota(i32, (PLANE, CAP, TOK), 1).astype(f32)
+    which = lax.broadcasted_iota(i32, (PLANE, TOK), 0)
+    expert_of = jnp.zeros((PLANE, TOK), i32)
+    for k in range(PLANE):
+        expert_of = jnp.where(which == k, match[z * PLANE + k], expert_of)
+    expert_of = expert_of.astype(f32)
 
     def select_of(slot):
         mask = jnp.zeros((PLANE, TOK), f32)
-        weight = jnp.zeros((PLANE, TOK), f32)
+        gates = jnp.zeros((PLANE, TOK), f32)
         top = meta.shape[0] // 2
         for k in range(top):
             hit = zm[slot, k:k + 1, :] == expert_of
             mask = jnp.where(hit, 1.0, mask)
-            weight = jnp.where(hit, zm[slot, top + k:top + k + 1, :], weight)
+            gates = jnp.where(hit, zm[slot, top + k:top + k + 1, :], gates)
         rank = jnp.dot(mask.astype(bf16), before, preferred_element_type=f32)
         rank = jnp.where(mask > 0.5, rank, -1.0)
         picked = jnp.where(rank[:, None, :] == place_of, 1.0, 0.0)
-        gate = jnp.sum(picked * weight[:, None, :], axis=2, keepdims=True)
+        gate = jnp.sum(picked * gates[:, None, :], axis=2, keepdims=True)
         return picked, gate
 
     def build(j):
@@ -174,6 +236,9 @@
         xt_own(j).start()
         for o in order:
             xt_copy(j, o).start()
+
+    landed = upb.at[y, own_rows, own_cols]
+    last_up = pltpu.make_async_copy(upout.at[e], landed, loc.at[1 + PAIRS + CHUNKS])
 
     for step in (1, 2, 3, 4):
         for d in (0, 1):
@@ -185,6 +250,43 @@
             if step < 4:
                 tok_copy(d, step + 1).start()
         send_tokens(0 if step == 4 else step)
+        if step == 2:
+            own_up.wait()
+            all_pieces(upmid, 0).wait_recv()
+
+            @pl.loop(0, TOTAL)
+            def _(i):
+                upout[i] = upmid[match[i]]
+
+            @pl.loop(1, TOTAL)
+            def _(o):
+                q = lax.rem(e + o, TOTAL)
+                remote(upout.at[q], landed, ex_s.at[2], ex_r.at[2], (y, q)).start()
+
+            last_up.start()
+            for c in range(CHUNKS):
+                cot_loads[c].wait()
+                for d in (0, 1):
+                    cot_copy(c, d, 1).start()
+
+    last_up.wait()
+    all_pieces(upout, 2).wait_recv()
+    for o in (2, 1, 3):
+        up_copy(o).start()
+
+    all_pieces(stg, 1).wait_send()
+    all_pieces(mid, 1).wait_recv()
+
+    @pl.loop(0, TOTAL)
+    def _(i):
+        stg[i] = mid[match[i]]
+
+    @pl.loop(1, TOTAL)
+    def _(o):
+        q = lax.rem(e + o, TOTAL)
+        remote(stg.at[q], fin.at[e], ex_s.at[3], ex_r.at[3], (y, q)).start()
+
+    fin[e] = stg[e]
 
     for step in (1, 2, 3, 4):
         for c in range(CHUNKS):
@@ -201,7 +303,6 @@
                 for o in order:
                     xc_copy(c, o).start()
 
-    own_up.wait()
     for o in range(1, NY):
         up_copy(o).wait_recv()
     for j in range(PAIRS):
@@ -239,11 +340,63 @@
         for o in (2, 1, 3):
             g_copy(c, o).start()
 
+    all_pieces(fin, 3).wait_recv()
+    norm[...] = jnp.zeros_like(norm)
+
+    def put(ref, c, slot):
+        return pltpu.make_async_copy(
+            gbuf.at[c, slot], ref.at[:, pl.ds(c * chunk, chunk)], store.at[c, slot])
+
     for c in range(CHUNKS):
         for o in range(1, NY):
-            g_copy(c, o).wait_recv()
-        summed = (gbuf[c, y] + grecv[c, 0]) + (grecv[c, 1] + grecv[c, 2])
-        out[:, c * chunk:(c + 1) * chunk] = summed
+            g_copy(c, o).wait()
+
+        @pl.loop(0, groups)
+        def _(g):
+            rows = pl.ds(pl.multiple_of(g * HIGH, HIGH), HIGH)
+            for h in range(per_chunk):
+                q = g * ACROSS + c * per_chunk + h
+                cols = slice(h * LANES, (h + 1) * LANES)
+                powers = fin[q, STATES * WORDS:].astype(f32)
+                scales = jnp.exp(powers * STEP) * (1.0 / LEVELS)
+
+                def state(a):
+                    word = fin[q, a * WORDS:(a + 1) * WORDS]
+                    upper = lax.shift_right_arithmetic(word, jnp.int32(16))
+                    lower = lax.bitwise_and(word, jnp.int32(65535)) - 32768
+                    return jnp.concatenate([upper, lower], axis=0).astype(f32) * scales[a:a + 1]
+
+                gradient = (gbuf[c, y, rows, cols] + grecv[c, 0, rows, cols]) + (
+                    grecv[c, 1, rows, cols] + grecv[c, 2, rows, cols])
+                old = state(0)
+                first = beta_one * state(1) + (1.0 - beta_one) * gradient
+                second = beta_two * state(2) + (1.0 - beta_two) * gradient * gradient
+                update = first / (jnp.sqrt(second) + epsilon)
+                gbuf[c, 0, rows, cols] = first
+                gbuf[c, 1, rows, cols] = second
+                gbuf[c, 2, rows, cols] = update
+                gbuf[c, 3, rows, cols] = old
+                norm[0:8] += jnp.sum((old * old).reshape(HIGH // 8, 8, LANES), axis=0)
+                norm[8:16] += jnp.sum((update * update).reshape(HIGH // 8, 8, LANES), axis=0)
+
+        put(new_1, c, 0).start()
+        put(new_2, c, 1).start()
+
+    def n_copy(o):
+        return remote(norm, norm_in.at[o - 1], n_s.at[o], n_r.at[o], layer(o)[1])
+
+    for o in range(1, NY):
+        n_copy(o).start()
+    for o in range(1, NY):
+        n_copy(o).wait_recv()
+    squares = (norm[...] + norm_in[0]) + (norm_in[1] + norm_in[2])
+    weight_sq = jnp.sum(jnp.sum(squares[0:8], axis=0, keepdims=True), axis=1, keepdims=True)
+    update_sq = jnp.sum(jnp.sum(squares[8:16], axis=0, keepdims=True), axis=1, keepdims=True)
+    trust = jnp.sqrt(weight_sq) / (jnp.sqrt(update_sq) + epsilon)
+    rate = learn_rate * trust
+    for c in range(CHUNKS):
+        gbuf[c, 3] = gbuf[c, 3] - rate * gbuf[c, 2]
+        put(new_w, c, 3).start()
 
     for step in (1, 2, 3, 4):
         for d in (0, 1):
@@ -252,18 +405,26 @@
             tok_copy(d, step).wait_send()
             for c in range(CHUNKS):
                 cot_copy(c, d, step).wait_send()
+    all_pieces(upmid, 0).wait_send()
+    all_pieces(upout, 2).wait_send()
+    all_pieces(stg, 3).wait_send()
     for o in range(1, NY):
         up_copy(o).wait_send()
-        for c in range(CHUNKS):
-            g_copy(c, o).wait_send()
+        n_copy(o).wait_send()
     for o in range(1, PLANE):
         for j in range(PAIRS):
             xt_copy(j, o).wait_send()
         for c in range(CHUNKS):
             xc_copy(c, o).wait_send()
-
-
-def expert_gradient(tokens, cotangent, expert_ids, gate_probs, up_weight):
+    for c in range(CHUNKS):
+        put(new_1, c, 0).wait()
+        put(new_2, c, 1).wait()
+        put(new_w, c, 3).wait()
+
+
+def local(
+    tokens, cotangent, expert_ids, gate_probs, up_weight, down_weight, moment1, moment2, pair_match
+):
     rows, width = tokens.shape
     chunk = width // CHUNKS
     units = up_weight.shape[2]
@@ -271,12 +432,16 @@
     meta = jnp.concatenate([expert_ids.astype(f32).T, gate_probs.T], axis=0)
     up = up_weight[0].T
     pick = PLANE * 2 * CAP
+    words = STATES * WORDS + 8
     dma = pltpu.SemaphoreType.DMA
-    return pl.pallas_call(
-        gradient_kernel,
-        out_shape=jax.ShapeDtypeStruct((units, width), f32),
-        in_specs=[pl.BlockSpec(memory_space=pltpu.VMEM)] * 4,
-        out_specs=pl.BlockSpec(memory_space=pltpu.VMEM),
+    anywhere = pl.BlockSpec(memory_space=pl.ANY)
+    outs = pl.pallas_call(
+        step_kernel,
+        out_shape=[jax.ShapeDtypeStruct((units, width), f32)] * 3,
+        in_specs=[
+            pl.BlockSpec(memory_space=pltpu.SMEM), pl.BlockSpec(memory_space=pltpu.VMEM),
+        ] + [anywhere] * 6,
+        out_specs=[anywhere] * 3,
         scratch_shapes=[
             pltpu.VMEM((NZ, rows, width), bf16),
             pltpu.VMEM((CHUNKS, NZ, rows, chunk), bf16),
@@ -291,6 +456,13 @@
             pltpu.VMEM((NY * units, PAIRS * pick), bf16),
             pltpu.VMEM((CHUNKS, NY, units, chunk), f32),
             pltpu.VMEM((CHUNKS, NY - 1, units, chunk), f32),
+            pltpu.VMEM((TOTAL, words, LANES), jnp.int32),
+            pltpu.VMEM((TOTAL, words, LANES), jnp.int32),
+            pltpu.VMEM((TOTAL, words, LANES), jnp.int32),
+            pltpu.VMEM((TOTAL, HIGH, LANES), bf16),
+            pltpu.VMEM((TOTAL, HIGH, LANES), bf16),
+            pltpu.VMEM((16, LANES), f32),
+            pltpu.VMEM((NY - 1, 16, LANES), f32),
             dma((2, 5)), dma((2, 5)),
             dma((2, 5)), dma((2, 5)),
             dma((CHUNKS, 2, 5)), dma((CHUNKS, 2, 5)),
@@ -298,64 +470,22 @@
             dma((PAIRS, PLANE)), dma((PAIRS, PLANE)),
             dma((CHUNKS, PLANE)), dma((CHUNKS, PLANE)),
             dma((CHUNKS, NY)), dma((CHUNKS, NY)),
-            dma((1 + PAIRS + CHUNKS,)),
+            dma((NY,)), dma((NY,)),
+            dma((4,)), dma((4,)),
+            dma((2 + PAIRS + CHUNKS,)),
+            dma((1 + CHUNKS + STATES * CHUNKS,)),
+            dma((CHUNKS, 4)),
         ],
         compiler_params=pltpu.CompilerParams(
-            collective_id=0, has_side_effects=True, vmem_limit_bytes=62 * 2**20
+            collective_id=0, has_side_effects=True, vmem_limit_bytes=VMEM_BYTES
         ),
         cost_estimate=pl.CostEstimate(
             flops=4 * PAIRS * pick * width * units * NY,
-            bytes_accessed=4 * rows * width + 2 * units * width * 3,
+            bytes_accessed=4 * rows * width + 26 * units * width,
             transcendentals=PAIRS * pick * units * NY,
         ),
-    )(tokens, cotangent, meta, up)
-
-
-def pick_kernel(match, src, out):
-    @pl.loop(0, src.shape[0])
-    def _(i):
-        out[i] = src[match[i]]
-
-
-def relocate(states, pair_match):
-    group_size = lax.axis_size("expert")
-    count = len(states)
-    rows, width = states[0].shape
-    high, lanes = rows // 4, 128
-    across = width // lanes
-    pieces = [s.reshape(4, high, across, lanes).transpose(0, 2, 1, 3) for s in states]
-    stacked = jnp.stack(pieces, axis=2).reshape(group_size, count * high, lanes)
-    spread = lax.all_to_all(stacked, "expert", split_axis=0, concat_axis=0, tiled=True)
-    chosen = pl.pallas_call(
-        pick_kernel,
-        out_shape=jax.ShapeDtypeStruct(spread.shape, spread.dtype),
-        in_specs=[pl.BlockSpec(memory_space=pltpu.SMEM), pl.BlockSpec(memory_space=pltpu.VMEM)],
-        out_specs=pl.BlockSpec(memory_space=pltpu.VMEM),
-        compiler_params=pltpu.CompilerParams(vmem_limit_bytes=32 * 2**20),
-    )(pair_match, spread)
-    arrived = lax.all_to_all(chosen, "expert", split_axis=0, concat_axis=0, tiled=True)
-    arrived = arrived.reshape(4, across, count, high, lanes).transpose(2, 0, 3, 1, 4)
-    arrived = arrived.reshape(count, rows, width)
-    return tuple(arrived[i] for i in range(count))
-
-
-def lamb_step(weight, moment_one, moment_two, gradient):
-    first = beta_one * moment_one + (1.0 - beta_one) * gradient
-    second = beta_two * moment_two + (1.0 - beta_two) * gradient * gradient
-    update = first / (jnp.sqrt(second) + epsilon)
-    weight_sq, update_sq = lax.psum((jnp.sum(weight * weight), jnp.sum(update * update)), "dp")
-    trust_ratio = jnp.sqrt(weight_sq) / (jnp.sqrt(update_sq) + epsilon)
-    renewed = weight - learn_rate * trust_ratio * update
-    return (renewed, first, second)
-
-
-def local(
-    tokens, cotangent, expert_ids, gate_probs, up_weight, down_weight, moment1, moment2, pair_match
-):
-    gradient = expert_gradient(tokens, cotangent, expert_ids, gate_probs, up_weight)
-    renewed, first, second = lamb_step(down_weight[0], moment1[0], moment2[0], gradient)
-    renewed, first, second = relocate((renewed, first, second), pair_match)
-    return (renewed[None], first[None], second[None])
+    )(pair_match, meta, tokens, cotangent, up, down_weight[0], moment1[0], moment2[0])
+    return tuple(out[None] for out in outs)
 
 
 def solution(mesh):

time: 460 us -> 351 us (0.76)
  blocking collectives: 238 us -> 0 us
  Pallas kernels: 195 us -> 342 us
  local copies, waits for them, and re-layouts: 14.8 us -> 5.94 us
  other arithmetic: 10.1 us -> 1.98 us
    all_to_all x2 -> x0, blocking collectives: 230 us -> none  [the longest x1 117 us: relocate(): lax.all_to_all(stacked, 'expert', split_axis=0, concat_axis=0, tiled=True)]
    pallas_call x2 -> x1, Pallas kernels: 195 us -> 342 us  [local(): pl.pallas_call(step_kernel, out_shape=[jax.ShapeDtypeStruct((units, width...]
    slice x7 -> x0, local copies, waits for them, and re-layouts: 10.6 us -> none  [relocate(): return tuple((arrived[i] for i in range(count)))]
    psum x1 -> x0, blocking collectives: 7.17 us -> none  [lamb_step(): lax.psum((jnp.sum(weight * weight), jnp.sum(update * update)), 'dp')]
    reduce_sum x1 -> x0, other arithmetic: 6.1 us -> none  [lamb_step(): jnp.sum(update * update)]
where the time goes in v2:
time: 351 us
  Pallas kernels  342 us (97%)
  local copies, waits for them, and re-layouts  5.94 us (2%)
    pallas_call x1, Pallas kernels, local(): pl.pallas_call(step_kernel, out_shape=[jax.ShapeDtypeStruct((units, width...  342 us

profile of v2, /device:TPU:1, one launch (start us, length us, event | category | flops | bytes accessed | tf_op | source)
XLA Modules:
  0.0 350.9 jit_solution(4932106598001016158)
XLA Ops:
  0.6 0.7 convert_bitcast_fusion
  1.3 1.3 pad_maximum_fusion.meta
  2.6 342.3 %shard_map.112 = (f32[192,2048]{1,0:T(8,128)}, f32[192,2048]{1,0:T(8,128)}, f32[192,2048]{1,0:T(8,128)}) custom-call(s32[64]{0:T(128)} %match.1, f32[16,128]{1,0:T(8,128)} %pad_maximum_fusion.meta, bf16[128,2048]{1,0:T(8,128)(2,1)} %tok.1, bf16[128,2048]{1,0:T(8,128)(2,1)} %cot.1, bf16[192,2048]{1,0:T(8,128)(2,1)} %bitcast.19, f32[192,2048]{1,0:T(8,128)} %bitcast.16, ...), custom_call_target="tpu_custom_call" | custom-call | flops 9663676416 | bytes 11272192 | tf_op jit(solution)/shard_map/pallas_call | solution.py:438
  344.9 0.0 copy-start.1
  344.9 2.8 copy.15
  347.8 0.0 copy-done.1
  347.8 0.0 copy-start
  347.8 1.1 copy.16
  348.9 0.8 copy-done
  349.7 1.1 copy.17
Async XLA Ops:
  344.9 2.8 copy-start.1
  347.8 2.0 copy-start

commit v3 on v2

--- a/solution.py
+++ b/solution.py
@@ -17,6 +17,8 @@
 TOK = 128
 PAIRS = NZ // 2
 CHUNKS = 4
+SPREAD_AFTER = 3
+GATHER_AFTER = 1
 VMEM_BYTES = 62 * 2**20
 TOTAL = NZ * PLANE
 HIGH, LANES = 48, 128
@@ -142,6 +144,11 @@
     own_up = pltpu.make_async_copy(up.at[own_rows, own_cols], upmid.at[e], loc.at[0])
     own_up.start()
 
+    for c in range(CHUNKS):
+        cot_loads[c].wait()
+        for d in (0, 1):
+            cot_copy(c, d, 1).start()
+
     scale_row = lax.broadcasted_iota(i32, (8, LANES), 0)
     for copy in state_loads:
         copy.wait()
@@ -162,13 +169,6 @@
                     powers = jnp.where(scale_row == a, power, powers)
                 stg[q, STATES * WORDS:] = powers.astype(i32)
 
-    @pl.loop(1, TOTAL)
-    def _(o):
-        q = lax.rem(e + o, TOTAL)
-        remote(stg.at[q], mid.at[e], ex_s.at[1], ex_r.at[1], (y, q)).start()
-
-    mid[e] = stg[e]
-
     def up_copy(o):
         k, device = layer(o)
         return remote(upb.at[y], upb.at[y], up_s.at[o], up_r.at[o], device)
@@ -264,29 +264,11 @@
                 remote(upout.at[q], landed, ex_s.at[2], ex_r.at[2], (y, q)).start()
 
             last_up.start()
-            for c in range(CHUNKS):
-                cot_loads[c].wait()
-                for d in (0, 1):
-                    cot_copy(c, d, 1).start()
 
     last_up.wait()
     all_pieces(upout, 2).wait_recv()
     for o in (2, 1, 3):
         up_copy(o).start()
-
-    all_pieces(stg, 1).wait_send()
-    all_pieces(mid, 1).wait_recv()
-
-    @pl.loop(0, TOTAL)
-    def _(i):
-        stg[i] = mid[match[i]]
-
-    @pl.loop(1, TOTAL)
-    def _(o):
-        q = lax.rem(e + o, TOTAL)
-        remote(stg.at[q], fin.at[e], ex_s.at[3], ex_r.at[3], (y, q)).start()
-
-    fin[e] = stg[e]
 
     for step in (1, 2, 3, 4):
         for c in range(CHUNKS):
@@ -302,6 +284,13 @@
                 xc_own(c).start()
                 for o in order:
                     xc_copy(c, o).start()
+        if step == SPREAD_AFTER:
+            @pl.loop(1, TOTAL)
+            def _(o):
+                q = lax.rem(e + o, TOTAL)
+                remote(stg.at[q], mid.at[e], ex_s.at[1], ex_r.at[1], (y, q)).start()
+
+            mid[e] = stg[e]
 
     for o in range(1, NY):
         up_copy(o).wait_recv()
@@ -339,6 +328,20 @@
 
         for o in (2, 1, 3):
             g_copy(c, o).start()
+        if c == GATHER_AFTER:
+            all_pieces(stg, 1).wait_send()
+            all_pieces(mid, 1).wait_recv()
+
+            @pl.loop(0, TOTAL)
+            def _(i):
+                stg[i] = mid[match[i]]
+
+            @pl.loop(1, TOTAL)
+            def _(o):
+                q = lax.rem(e + o, TOTAL)
+                remote(stg.at[q], fin.at[e], ex_s.at[3], ex_r.at[3], (y, q)).start()
+
+            fin[e] = stg[e]
 
     all_pieces(fin, 3).wait_recv()
     norm[...] = jnp.zeros_like(norm)

time: 351 us -> 287 us (0.82)
  Pallas kernels: 342 us -> 278 us
    pallas_call x1, Pallas kernels: 342 us -> 278 us  [local(): pl.pallas_call(step_kernel, out_shape=[jax.ShapeDtypeStruct((units, width...]
where the time goes in v3:
time: 287 us
  Pallas kernels  278 us (97%)
  local copies, waits for them, and re-layouts  5.94 us (2%)
    pallas_call x1, Pallas kernels, local(): pl.pallas_call(step_kernel, out_shape=[jax.ShapeDtypeStruct((units, width...  278 us
    unnamed x7, local copies, waits for them, and re-layouts  5.94 us

profile of v3, /device:TPU:1, one launch (start us, length us, event | category | flops | bytes accessed | tf_op | source)
XLA Modules:
  0.0 286.8 jit_solution(4481514378620122833)
XLA Ops:
  0.6 0.7 convert_bitcast_fusion
  1.3 1.3 pad_maximum_fusion.meta
  2.6 278.2 %shard_map.112 = (f32[192,2048]{1,0:T(8,128)}, f32[192,2048]{1,0:T(8,128)}, f32[192,2048]{1,0:T(8,128)}) custom-call(s32[64]{0:T(128)} %match.1, f32[16,128]{1,0:T(8,128)} %pad_maximum_fusion.meta, bf16[128,2048]{1,0:T(8,128)(2,1)} %tok.1, bf16[128,2048]{1,0:T(8,128)(2,1)} %cot.1, bf16[192,2048]{1,0:T(8,128)(2,1)} %bitcast.19, f32[192,2048]{1,0:T(8,128)} %bitcast.16, ...), custom_call_target="tpu_custom_call" | custom-call | flops 9663676416 | bytes 11272192 | tf_op jit(solution)/shard_map/pallas_call | solution.py:441
  280.8 0.0 copy-start.1
  280.8 2.8 copy.15
  283.6 0.0 copy-done.1
  283.6 0.0 copy-start
  283.6 1.1 copy.16
  284.8 0.8 copy-done
  285.6 1.1 copy.17
Async XLA Ops:
  280.8 2.8 copy-start.1
  283.6 2.0 copy-start

commit v4 on v3

--- a/solution.py
+++ b/solution.py
@@ -16,9 +16,11 @@
 CAP = 24
 TOK = 128
 PAIRS = NZ // 2
-CHUNKS = 4
+CHUNKS = 8
+RING = 4
+PARTS = 2
 SPREAD_AFTER = 3
-GATHER_AFTER = 1
+GATHER_AFTER = 3
 VMEM_BYTES = 62 * 2**20
 TOTAL = NZ * PLANE
 HIGH, LANES = 48, 128
@@ -41,6 +43,8 @@
     width = tok.shape[1]
     chunk = width // CHUNKS
     per_chunk = chunk // LANES
+    ring_cols = width // RING
+    part = width // PARTS
     slice_rows = up.shape[0]
     groups = slice_rows // HIGH
     y = lax.axis_index("dp")
@@ -58,15 +62,22 @@
         k = lax.rem(y + o, NY)
         return k, (k, e)
 
-    tok_load = pltpu.make_async_copy(tok, zt.at[0], load.at[0])
-    tok_load.start()
+    tok_loads = [
+        pltpu.make_async_copy(tok.at[:, pl.ds(t * part, part)], zt.at[t, 0], load.at[t])
+        for t in range(PARTS)
+    ]
+    for copy in tok_loads:
+        copy.start()
     cot_loads = [
-        pltpu.make_async_copy(cot.at[:, pl.ds(c * chunk, chunk)], zc.at[c, 0], load.at[1 + c])
-        for c in range(CHUNKS)
+        pltpu.make_async_copy(
+            cot.at[:, pl.ds(c * ring_cols, ring_cols)], zc.at[c, 0], load.at[PARTS + c])
+        for c in range(RING)
     ]
     state_loads = [
         pltpu.make_async_copy(
-            ref.at[:, pl.ds(c * chunk, chunk)], gbuf.at[a, c], load.at[1 + CHUNKS + a * CHUNKS + c])
+            ref.at[:, pl.ds(c * chunk, chunk)],
+            gbuf.at[(a * CHUNKS + c) // NY, (a * CHUNKS + c) % NY],
+            load.at[PARTS + RING + a * CHUNKS + c])
         for a, ref in enumerate((weight, moment1, moment2)) for c in range(CHUNKS)
     ]
     for copy in state_loads + cot_loads:
@@ -106,8 +117,8 @@
         return remote(src, dst, send.at[direction, step], recv.at[direction, step],
                       left if direction else right)
 
-    def tok_copy(direction, step):
-        return z_copy(zt, zt_s, zt_r, direction, step)
+    def tok_copy(t, direction, step):
+        return z_copy(zt.at[t], zt_s.at[t], zt_r.at[t], direction, step)
 
     def cot_copy(c, direction, step):
         return z_copy(zc.at[c], zc_s.at[c], zc_r.at[c], direction, step)
@@ -120,10 +131,12 @@
     def meta_steps(step):
         return (0,) if step == 4 else (0, 1)
 
-    tok_load.wait()
     for d in (0, 1):
         meta_copy(d, 1).start()
-        tok_copy(d, 1).start()
+    for t in range(PARTS):
+        tok_loads[t].wait()
+        for d in (0, 1):
+            tok_copy(t, d, 1).start()
 
     def piece_of(q):
         rows = pl.ds(pl.multiple_of((q // ACROSS) * HIGH, HIGH), HIGH)
@@ -144,7 +157,7 @@
     own_up = pltpu.make_async_copy(up.at[own_rows, own_cols], upmid.at[e], loc.at[0])
     own_up.start()
 
-    for c in range(CHUNKS):
+    for c in range(RING):
         cot_loads[c].wait()
         for d in (0, 1):
             cot_copy(c, d, 1).start()
@@ -160,7 +173,7 @@
                 q = g * ACROSS + c * per_chunk + h
                 powers = jnp.zeros((8, LANES), f32)
                 for a in range(STATES):
-                    x = gbuf[a, c, g * HIGH:(g + 1) * HIGH, h * LANES:(h + 1) * LANES]
+                    x = gbuf[(a * CHUNKS + c) // NY, lax.rem(a * CHUNKS + c, NY), g * HIGH:(g + 1) * HIGH, h * LANES:(h + 1) * LANES]
                     most = jnp.maximum(jnp.max(jnp.abs(x), axis=0, keepdims=True), 1e-30)
                     power = jnp.ceil(jnp.log(most) * (1.0 / STEP))
                     inverse = 1.0 / (jnp.exp(power * STEP) * (1.0 / LEVELS))
@@ -207,9 +220,11 @@
         sel[j] = both.reshape(PLANE * 2 * CAP, 2 * TOK).astype(bf16)
         prob[j] = jnp.concatenate([first_gate, second_gate], axis=1).reshape(PLANE * 2 * CAP, 1)
 
-    def xt_copy(j, o):
+    def xt_copy(j, t, o):
         q, device = mate(o)
-        return remote(sbt.at[j, q], rbt.at[p, j], xt_s.at[j, o], xt_r.at[j, o], device)
+        cols = pl.ds(t * part, part)
+        return remote(sbt.at[j, q, :, cols], rbt.at[p, j, :, cols],
+                      xt_s.at[j, t, o], xt_r.at[j, t, o], device)
 
     def xt_own(j):
         return pltpu.make_async_copy(sbt.at[j, p], rbt.at[p, j], loc.at[1 + j])
@@ -223,19 +238,17 @@
 
     order = (4, 2, 6, 3, 5, 1, 7)
 
-    def send_tokens(j):
-        build(j)
-
-        @pl.loop(0, CHUNKS)
+    def send_tokens(j, t):
+        @pl.loop(0, part // 512)
         def _(c):
-            cols = pl.ds(pl.multiple_of(c * chunk, chunk), chunk)
-            pair = zt[2 * j:2 * j + 2, :, cols].reshape(2 * TOK, chunk)
+            cols = pl.ds(pl.multiple_of(c * 512, 512), 512)
+            pair = zt[t, 2 * j:2 * j + 2, :, cols].reshape(2 * TOK, 512)
             rows = jnp.dot(sel[j], pair, preferred_element_type=f32)
-            sbt[j, :, :, cols] = rows.astype(bf16).reshape(PLANE, 2 * CAP, chunk)
-
-        xt_own(j).start()
+            there = pl.ds(pl.multiple_of(t * part + c * 512, 512), 512)
+            sbt[j, :, :, there] = rows.astype(bf16).reshape(PLANE, 2 * CAP, 512)
+
         for o in order:
-            xt_copy(j, o).start()
+            xt_copy(j, t, o).start()
 
     landed = upb.at[y, own_rows, own_cols]
     last_up = pltpu.make_async_copy(upout.at[e], landed, loc.at[1 + PAIRS + CHUNKS])
@@ -246,10 +259,16 @@
                 meta_copy(d, step).wait_recv()
                 if step < 4 and d in meta_steps(step + 1):
                     meta_copy(d, step + 1).start()
-            tok_copy(d, step).wait_recv()
-            if step < 4:
-                tok_copy(d, step + 1).start()
-        send_tokens(0 if step == 4 else step)
+        j = 0 if step == 4 else step
+        for t in range(PARTS):
+            for d in (0, 1):
+                tok_copy(t, d, step).wait_recv()
+                if step < 4:
+                    tok_copy(t, d, step + 1).start()
+            if t == 0:
+                build(j)
+            send_tokens(j, t)
+        xt_own(j).start()
         if step == 2:
             own_up.wait()
             all_pieces(upmid, 0).wait_recv()
@@ -271,14 +290,16 @@
         up_copy(o).start()
 
     for step in (1, 2, 3, 4):
-        for c in range(CHUNKS):
+        for r in range(RING):
             for d in (0, 1):
-                cot_copy(c, d, step).wait_recv()
+                cot_copy(r, d, step).wait_recv()
                 if step < 4:
-                    cot_copy(c, d, step + 1).start()
-            if step == 4:
+                    cot_copy(r, d, step + 1).start()
+            ratio = CHUNKS // RING
+            for c in range(r * ratio, (r + 1) * ratio) if step == 4 else ():
+                across = slice((c % ratio) * chunk, (c % ratio + 1) * chunk)
                 for j in range(PAIRS):
-                    pair = zc[c, 2 * j:2 * j + 2].reshape(2 * TOK, chunk)
+                    pair = zc[r, 2 * j:2 * j + 2, :, across].reshape(2 * TOK, chunk)
                     rows = jnp.dot(sel[j], pair, preferred_element_type=f32) * prob[j]
                     sbs[c, :, j] = rows.astype(bf16).reshape(PLANE, 2 * CAP, chunk)
                 xc_own(c).start()
@@ -297,7 +318,8 @@
     for j in range(PAIRS):
         xt_own(j).wait()
         for o in range(1, PLANE):
-            xt_copy(j, o).wait_recv()
+            for t in range(PARTS):
+                xt_copy(j, t, o).wait_recv()
     span = 2 * PAIRS * 2 * CAP
 
     @pl.loop(0, PLANE // 2)
@@ -405,8 +427,9 @@
         for d in (0, 1):
             if d in meta_steps(step):
                 meta_copy(d, step).wait_send()
-            tok_copy(d, step).wait_send()
-            for c in range(CHUNKS):
+            for t in range(PARTS):
+                tok_copy(t, d, step).wait_send()
+            for c in range(RING):
                 cot_copy(c, d, step).wait_send()
     all_pieces(upmid, 0).wait_send()
     all_pieces(upout, 2).wait_send()
@@ -416,7 +439,8 @@
         n_copy(o).wait_send()
     for o in range(1, PLANE):
         for j in range(PAIRS):
-            xt_copy(j, o).wait_send()
+            for t in range(PARTS):
+                xt_copy(j, t, o).wait_send()
         for c in range(CHUNKS):
             xc_copy(c, o).wait_send()
     for c in range(CHUNKS):
@@ -446,8 +470,8 @@
         ] + [anywhere] * 6,
         out_specs=[anywhere] * 3,
         scratch_shapes=[
-            pltpu.VMEM((NZ, rows, width), bf16),
-            pltpu.VMEM((CHUNKS, NZ, rows, chunk), bf16),
+            pltpu.VMEM((PARTS, NZ, rows, width // PARTS), bf16),
+            pltpu.VMEM((RING, NZ, rows, width // RING), bf16),
             pltpu.VMEM((NZ,) + meta.shape, f32),
             pltpu.VMEM((PAIRS, pick, 2 * rows), bf16),
             pltpu.VMEM((PAIRS, pick, 1), f32),
@@ -466,17 +490,17 @@
             pltpu.VMEM((TOTAL, HIGH, LANES), bf16),
             pltpu.VMEM((16, LANES), f32),
             pltpu.VMEM((NY - 1, 16, LANES), f32),
+            dma((PARTS, 2, 5)), dma((PARTS, 2, 5)),
             dma((2, 5)), dma((2, 5)),
-            dma((2, 5)), dma((2, 5)),
-            dma((CHUNKS, 2, 5)), dma((CHUNKS, 2, 5)),
+            dma((RING, 2, 5)), dma((RING, 2, 5)),
             dma((NY,)), dma((NY,)),
-            dma((PAIRS, PLANE)), dma((PAIRS, PLANE)),
+            dma((PAIRS, PARTS, PLANE)), dma((PAIRS, PARTS, PLANE)),
             dma((CHUNKS, PLANE)), dma((CHUNKS, PLANE)),
             dma((CHUNKS, NY)), dma((CHUNKS, NY)),
             dma((NY,)), dma((NY,)),
             dma((4,)), dma((4,)),
             dma((2 + PAIRS + CHUNKS,)),
-            dma((1 + CHUNKS + STATES * CHUNKS,)),
+            dma((PARTS + RING + STATES * CHUNKS,)),
             dma((CHUNKS, 4)),
         ],
         compiler_params=pltpu.CompilerParams(

time: 287 us -> 280 us (0.976)
  Pallas kernels: 278 us -> 270 us
    pallas_call x1, Pallas kernels: 278 us -> 270 us  [local(): pl.pallas_call(step_kernel, out_shape=[jax.ShapeDtypeStruct((units, width...]
where the time goes in v4:
time: 280 us; the launch traced here: 279 us
  Pallas kernels  270 us (96%)
  local copies, waits for them, and re-layouts  5.94 us (2%)
    pallas_call x1, Pallas kernels, local(): pl.pallas_call(step_kernel, out_shape=[jax.ShapeDtypeStruct((units, width...  270 us
    unnamed x7, local copies, waits for them, and re-layouts  5.94 us

profile of v4, /device:TPU:1, one launch (start us, length us, event | category | flops | bytes accessed | tf_op | source)
XLA Modules:
  0.0 278.8 jit_solution(12346868335513053651)
XLA Ops:
  0.6 0.7 convert_bitcast_fusion
  1.3 1.3 pad_maximum_fusion.meta
  2.6 270.3 %shard_map.112 = (f32[192,2048]{1,0:T(8,128)}, f32[192,2048]{1,0:T(8,128)}, f32[192,2048]{1,0:T(8,128)}) custom-call(s32[64]{0:T(128)} %match.1, f32[16,128]{1,0:T(8,128)} %pad_maximum_fusion.meta, bf16[128,2048]{1,0:T(8,128)(2,1)} %tok.1, bf16[128,2048]{1,0:T(8,128)(2,1)} %cot.1, bf16[192,2048]{1,0:T(8,128)(2,1)} %bitcast.19, f32[192,2048]{1,0:T(8,128)} %bitcast.16, ...), custom_call_target="tpu_custom_call" | custom-call | flops 9663676416 | bytes 11272192 | tf_op jit(solution)/shard_map/pallas_call | solution.py:465
  272.9 0.0 copy-start.1
  272.9 2.8 %copy.15 = f32[1,192,2048]{2,1,0:T(8,128)} copy(f32[1,192,2048]{2,1,0:T(8,128)} %bitcast.14) | data formatting | bytes 3145728
  275.7 0.0 copy-done.1
  275.7 0.0 copy-start
  275.7 1.1 copy.16
  276.9 0.8 copy-done
  277.7 1.1 copy.17
Async XLA Ops:
  272.9 2.8 %copy-start.1 = (f32[192,2048]{1,0:T(8,128)S(1)}, f32[192,2048]{1,0:T(8,128)}, u32[]{:S(2)}) copy-start(f32[192,2048]{1,0:T(8,128)} %get-tuple-element.7) | copy-start | bytes 4718596
  275.7 2.0 copy-start

commit v5 on v4

--- a/solution.py
+++ b/solution.py
@@ -29,11 +29,12 @@
 STATES = 3
 STEP = 0.6931471805599453 / 8.0
 LEVELS = 32767.0
+SMALLEST = 2.0**-63
 MESH = pl.DeviceIdType.MESH
 
 
 def step_kernel(
-    match, meta, tok, cot, up, weight, moment1, moment2, new_w, new_1, new_2,
+    match, ids, gates, tok, cot, up, weight, moment1, moment2, new_w, new_1, new_2,
     zt, zc, zm, sel, prob, sbt, sbs, rbt, rbs, upb, hid, gbuf, grecv,
     stg, mid, fin, upmid, upout, norm, norm_in,
     zt_s, zt_r, zm_s, zm_r, zc_s, zc_r, up_s, up_r, xt_s, xt_r, xc_s, xc_r, g_s, g_r, n_s, n_r,
@@ -82,7 +83,9 @@
     ]
     for copy in state_loads + cot_loads:
         copy.start()
-    zm[0] = meta[...]
+    top = ids.shape[0]
+    zm[0, 0:top] = ids[...].astype(f32)
+    zm[0, top:] = gates[...]
 
     barrier = pltpu.get_barrier_semaphore()
 
@@ -157,12 +160,6 @@
     own_up = pltpu.make_async_copy(up.at[own_rows, own_cols], upmid.at[e], loc.at[0])
     own_up.start()
 
-    for c in range(RING):
-        cot_loads[c].wait()
-        for d in (0, 1):
-            cot_copy(c, d, 1).start()
-
-    scale_row = lax.broadcasted_iota(i32, (8, LANES), 0)
     for copy in state_loads:
         copy.wait()
 
@@ -171,16 +168,16 @@
         for h in range(per_chunk):
             for g in range(groups):
                 q = g * ACROSS + c * per_chunk + h
-                powers = jnp.zeros((8, LANES), f32)
+                powers = jnp.zeros((1, LANES), i32)
                 for a in range(STATES):
                     x = gbuf[(a * CHUNKS + c) // NY, lax.rem(a * CHUNKS + c, NY), g * HIGH:(g + 1) * HIGH, h * LANES:(h + 1) * LANES]
-                    most = jnp.maximum(jnp.max(jnp.abs(x), axis=0, keepdims=True), 1e-30)
+                    most = jnp.maximum(jnp.max(jnp.abs(x), axis=0, keepdims=True), SMALLEST)
                     power = jnp.ceil(jnp.log(most) * (1.0 / STEP))
                     inverse = 1.0 / (jnp.exp(power * STEP) * (1.0 / LEVELS))
                     code = jnp.clip(jnp.floor(x * inverse + 0.5), -LEVELS, LEVELS).astype(i32)
                     stg[q, a * WORDS:(a + 1) * WORDS] = code[:WORDS] * 65536 + (code[WORDS:] + 32768)
-                    powers = jnp.where(scale_row == a, power, powers)
-                stg[q, STATES * WORDS:] = powers.astype(i32)
+                    powers = powers + (power.astype(i32) + 512) * 1024 ** a
+                stg[q, STATES * WORDS:] = powers
 
     def up_copy(o):
         k, device = layer(o)
@@ -198,16 +195,15 @@
 
     def select_of(slot):
         mask = jnp.zeros((PLANE, TOK), f32)
-        gates = jnp.zeros((PLANE, TOK), f32)
-        top = meta.shape[0] // 2
+        weights = jnp.zeros((PLANE, TOK), f32)
         for k in range(top):
             hit = zm[slot, k:k + 1, :] == expert_of
             mask = jnp.where(hit, 1.0, mask)
-            gates = jnp.where(hit, zm[slot, top + k:top + k + 1, :], gates)
+            weights = jnp.where(hit, zm[slot, top + k:top + k + 1, :], weights)
         rank = jnp.dot(mask.astype(bf16), before, preferred_element_type=f32)
         rank = jnp.where(mask > 0.5, rank, -1.0)
         picked = jnp.where(rank[:, None, :] == place_of, 1.0, 0.0)
-        gate = jnp.sum(picked * gates[:, None, :], axis=2, keepdims=True)
+        gate = jnp.sum(picked * weights[:, None, :], axis=2, keepdims=True)
         return picked, gate
 
     def build(j):
@@ -269,6 +265,11 @@
                 build(j)
             send_tokens(j, t)
         xt_own(j).start()
+        if step == 2:
+            for c in range(RING):
+                cot_loads[c].wait()
+                for d in (0, 1):
+                    cot_copy(c, d, 1).start()
         if step == 2:
             own_up.wait()
             all_pieces(upmid, 0).wait_recv()
@@ -382,14 +383,16 @@
             for h in range(per_chunk):
                 q = g * ACROSS + c * per_chunk + h
                 cols = slice(h * LANES, (h + 1) * LANES)
-                powers = fin[q, STATES * WORDS:].astype(f32)
-                scales = jnp.exp(powers * STEP) * (1.0 / LEVELS)
+                powers = fin[q, STATES * WORDS:]
 
                 def state(a):
                     word = fin[q, a * WORDS:(a + 1) * WORDS]
                     upper = lax.shift_right_arithmetic(word, jnp.int32(16))
                     lower = lax.bitwise_and(word, jnp.int32(65535)) - 32768
-                    return jnp.concatenate([upper, lower], axis=0).astype(f32) * scales[a:a + 1]
+                    field = lax.shift_right_arithmetic(powers, jnp.int32(10 * a))
+                    power = (lax.bitwise_and(field, jnp.int32(1023)) - 512).astype(f32)
+                    scale = jnp.exp(power * STEP) * (1.0 / LEVELS)
+                    return jnp.concatenate([upper, lower], axis=0).astype(f32) * scale
 
                 gradient = (gbuf[c, y, rows, cols] + grecv[c, 0, rows, cols]) + (
                     grecv[c, 1, rows, cols] + grecv[c, 2, rows, cols])
@@ -456,23 +459,24 @@
     chunk = width // CHUNKS
     units = up_weight.shape[2]
     bf16, f32 = jnp.bfloat16, jnp.float32
-    meta = jnp.concatenate([expert_ids.astype(f32).T, gate_probs.T], axis=0)
+    ids, gates = expert_ids.T, gate_probs.T
     up = up_weight[0].T
     pick = PLANE * 2 * CAP
-    words = STATES * WORDS + 8
+    words = STATES * WORDS + 1
     dma = pltpu.SemaphoreType.DMA
     anywhere = pl.BlockSpec(memory_space=pl.ANY)
     outs = pl.pallas_call(
         step_kernel,
         out_shape=[jax.ShapeDtypeStruct((units, width), f32)] * 3,
         in_specs=[
-            pl.BlockSpec(memory_space=pltpu.SMEM), pl.BlockSpec(memory_space=pltpu.VMEM),
+            pl.BlockSpec(memory_space=pltpu.SMEM),
+            pl.BlockSpec(memory_space=pltpu.VMEM), pl.BlockSpec(memory_space=pltpu.VMEM),
         ] + [anywhere] * 6,
         out_specs=[anywhere] * 3,
         scratch_shapes=[
             pltpu.VMEM((PARTS, NZ, rows, width // PARTS), bf16),
             pltpu.VMEM((RING, NZ, rows, width // RING), bf16),
-            pltpu.VMEM((NZ,) + meta.shape, f32),
+            pltpu.VMEM((NZ, 2 * ids.shape[0], rows), f32),
             pltpu.VMEM((PAIRS, pick, 2 * rows), bf16),
             pltpu.VMEM((PAIRS, pick, 1), f32),
             pltpu.VMEM((PAIRS, PLANE, 2 * CAP, width), bf16),
@@ -511,7 +515,7 @@
             bytes_accessed=4 * rows * width + 26 * units * width,
             transcendentals=PAIRS * pick * units * NY,
         ),
-    )(pair_match, meta, tokens, cotangent, up, down_weight[0], moment1[0], moment2[0])
+    )(pair_match, ids, gates, tokens, cotangent, up, down_weight[0], moment1[0], moment2[0])
     return tuple(out[None] for out in outs)
 
 

time: 280 us -> 273 us (0.975)
  Pallas kernels: 270 us -> 266 us
    pallas_call x1, Pallas kernels: 270 us -> 266 us  [local(): pl.pallas_call(step_kernel, out_shape=[jax.ShapeDtypeStruct((units, width...]
where the time goes in v5:
time: 273 us
  Pallas kernels  266 us (97%)
  local copies, waits for them, and re-layouts  5.94 us (2%)
    pallas_call x1, Pallas kernels, local(): pl.pallas_call(step_kernel, out_shape=[jax.ShapeDtypeStruct((units, width...  266 us
    unnamed x7, local copies, waits for them, and re-layouts  5.94 us

profile of v5, /device:TPU:1, one launch (start us, length us, event | category | flops | bytes accessed | tf_op | source)
XLA Modules:
  0.0 272.6 jit_solution(14979065603106038734)
XLA Ops:
  0.6 266.0 %shard_map.112 = (f32[192,2048]{1,0:T(8,128)}, f32[192,2048]{1,0:T(8,128)}, f32[192,2048]{1,0:T(8,128)}) custom-call(s32[64]{0:T(128)} %match.1, s32[8,128]{1,0:T(8,128)} %bitcast.18, f32[8,128]{1,0:T(8,128)} %bitcast.19, bf16[128,2048]{1,0:T(8,128)(2,1)} %tok.1, bf16[128,2048]{1,0:T(8,128)(2,1)} %cot.1, bf16[192,2048]{1,0:T(8,128)(2,1)} %bitcast.17, ...), custom_call_target="tpu_custom_call" | custom-call | flops 9663676416 | bytes 11272192 | tf_op jit(solution)/shard_map/pallas_call | solution.py:468
  266.6 0.0 copy-start.1
  266.6 2.8 %copy.15 = f32[1,192,2048]{2,1,0:T(8,128)} copy(f32[1,192,2048]{2,1,0:T(8,128)} %bitcast.13) | data formatting | bytes 3145728
  269.4 0.0 copy-done.1
  269.4 0.0 copy-start
  269.4 1.1 copy.16
  270.6 0.8 copy-done
  271.4 1.1 copy.17
Async XLA Ops:
  266.6 2.8 %copy-start.1 = (f32[192,2048]{1,0:T(8,128)S(1)}, f32[192,2048]{1,0:T(8,128)}, u32[]{:S(2)}) copy-start(f32[192,2048]{1,0:T(8,128)} %get-tuple-element.7) | copy-start | bytes 4718596
  269.4 2.0 copy-start

commit v6 on v5

--- a/solution.py
+++ b/solution.py
@@ -20,7 +20,7 @@
 RING = 4
 PARTS = 2
 SPREAD_AFTER = 3
-GATHER_AFTER = 3
+GATHER_AFTER = 4
 VMEM_BYTES = 62 * 2**20
 TOTAL = NZ * PLANE
 HIGH, LANES = 48, 128
@@ -265,7 +265,7 @@
                 build(j)
             send_tokens(j, t)
         xt_own(j).start()
-        if step == 2:
+        if step == 3:
             for c in range(RING):
                 cot_loads[c].wait()
                 for d in (0, 1):

time: 273 us -> 270 us (0.989); the launches traced: 273 us -> 266 us
  Pallas kernels: 266 us -> 259 us
    pallas_call x1, Pallas kernels: 266 us -> 259 us  [local(): pl.pallas_call(step_kernel, out_shape=[jax.ShapeDtypeStruct((units, width...]
where the time goes in v6:
time: 270 us; the launch traced here: 266 us
  Pallas kernels  259 us (96%)
  local copies, waits for them, and re-layouts  5.94 us (2%)
    pallas_call x1, Pallas kernels, local(): pl.pallas_call(step_kernel, out_shape=[jax.ShapeDtypeStruct((units, width...  259 us
    unnamed x7, local copies, waits for them, and re-layouts  5.94 us

profile of v6, /device:TPU:1, one launch (start us, length us, event | category | flops | bytes accessed | tf_op | source)
XLA Modules:
  0.0 265.9 jit_solution(9499645054007831770)
XLA Ops:
  0.6 259.3 %shard_map.112 = (f32[192,2048]{1,0:T(8,128)}, f32[192,2048]{1,0:T(8,128)}, f32[192,2048]{1,0:T(8,128)}) custom-call(s32[64]{0:T(128)} %match.1, s32[8,128]{1,0:T(8,128)} %bitcast.18, f32[8,128]{1,0:T(8,128)} %bitcast.19, bf16[128,2048]{1,0:T(8,128)(2,1)} %tok.1, bf16[128,2048]{1,0:T(8,128)(2,1)} %cot.1, bf16[192,2048]{1,0:T(8,128)(2,1)} %bitcast.17, ...), custom_call_target="tpu_custom_call" | custom-call | flops 9663676416 | bytes 11272192 | tf_op jit(solution)/shard_map/pallas_call | solution.py:468
  260.0 0.0 copy-start.1
  260.0 2.8 %copy.15 = f32[1,192,2048]{2,1,0:T(8,128)} copy(f32[1,192,2048]{2,1,0:T(8,128)} %bitcast.13) | data formatting | bytes 3145728
  262.8 0.0 copy-done.1
  262.8 0.0 copy-start
  262.8 1.1 copy.16
  263.9 0.8 copy-done
  264.8 1.1 copy.17
Async XLA Ops:
  260.0 2.8 %copy-start.1 = (f32[192,2048]{1,0:T(8,128)S(1)}, f32[192,2048]{1,0:T(8,128)}, u32[]{:S(2)}) copy-start(f32[192,2048]{1,0:T(8,128)} %get-tuple-element.7) | copy-start | bytes 4718596
  262.8 2.0 copy-start
